TPU v7x, 32 devices: a whole 2x2x4 slice. The times are simulated.
32 devices in a mesh: sky: 4 (over y, x), epoch: 8 (over z, core).
Axes of the slice: x: 2, y: 2, z: 4, core: 2. Of those that a mesh axis runs over, the one named last changes fastest.
Arguments:
- params: bfloat16 [512, 64], P('sky'), may hold values from -6 to 6
- basis: bfloat16 [64, 4096], replicated, may hold values from -0.75 to 0.75
- psf_taps: float32 [8, 2, 51], P('epoch'), may hold values from 0.02 to 1
- send_index: int32 [4, 4, 16], P('sky'), may hold values from 0 to 127
- tile_count: int32 [4, 4], P('sky'), may hold values from 0 to 16, as said below
- stamp_row: int32 [4, 4, 16], P('sky'), may hold values from 0 to 256
- stamp_col: int32 [4, 4, 16], P('sky'), may hold values from 0 to 448
- observed: float32 [8, 1024, 512], P('epoch', 'sky'), may hold values from 0 to 6
- background: float32 [8, 1024, 512], P('epoch', 'sky'), may hold values from 0.5 to 2
Outputs:
- param_grad: float32 [512, 64], P('sky')
- residual: float32 [8, 1024, 512], P('epoch', 'sky')
Inputs may be any that keep to these rules, and one draw needn't show every extreme that they name: `send_index`: slots with k >= tile_count[t, o] are dead and may name any row; they still lie within range. `tile_count`: some tiles are crowded and receive nearly 16 slots from every owner; in every draw at least one tile receives exactly 16 from owner 0. `stamp_row`: A stamp lies inside its tile's canvas.
All inputs are finite; a program needn't handle non-finite values.
Results may differ from a plain program's by a relative error of at most 0.0003.
Values may be sent and summed in bfloat16 or wider, within the bound.
A program may use at most 64 MiB of HBM per device.

v0:
```python
import math

import jax
import jax.numpy as jnp
from jax import lax
from jax.sharding import PartitionSpec as P


def extended_2(cells, sides, width):
    for axis, dim in sides:
        count = lax.axis_size(axis)
        ends = count - 1
        head = lax.slice_in_dim(cells, 0, width, axis=dim)
        tail = lax.slice_in_dim(cells, cells.shape[dim] - width, cells.shape[dim], axis=dim)
        cells = jnp.concatenate(
            [
                lax.ppermute(tail, axis, [(i, (i + 1) % count) for i in range(ends)]),
                cells,
                lax.ppermute(head, axis, [((i + 1) % count, i) for i in range(ends)]),
            ],
            axis=dim,
        )
    return cells


def toeplitz(taps, width):
    half = (taps.shape[0] - 1) // 2
    rows_at = jnp.arange(width, dtype=jnp.int32)[:, None]
    cols_at = jnp.arange(width, dtype=jnp.int32)[None, :]
    where_at = rows_at - cols_at + half
    inside = (where_at >= 0) & (where_at < taps.shape[0])
    return jnp.where(
        inside, taps[jnp.clip(where_at, 0, taps.shape[0] - 1)], jnp.zeros((), taps.dtype)
    )


def on_device(
    params, basis, psf_taps, send_index, tile_count, stamp_row, stamp_col, observed, background
):
    highest = lax.Precision.HIGHEST
    stamp_size = math.isqrt(basis.shape[1])
    margin = stamp_size // 2
    n_sky = send_index.shape[1]
    capacity = send_index.shape[2]
    slots = n_sky * capacity
    tile_rows = observed.shape[1]
    width = observed.shape[2]
    canvas_rows = tile_rows + 2 * margin
    taps = psf_taps[0] / jnp.sum(psf_taps[0], axis=-1, keepdims=True)
    row_kernel = toeplitz(taps[0], stamp_size)
    col_kernel = toeplitz(taps[1], stamp_size)
    basis_wide = basis.astype(jnp.float32).T
    live = jnp.arange(capacity, dtype=jnp.int32)[None, :] < tile_count[0][:, None]
    live_flat = live.reshape(slots, 1)
    outgoing = params[send_index[0]]
    intrinsic = jnp.dot(outgoing.reshape(slots, -1), basis, preferred_element_type=jnp.float32)
    intrinsic = intrinsic.reshape(-1, stamp_size, stamp_size)
    rendered = jnp.einsum("ab,nbc,dc->nad", row_kernel, intrinsic, col_kernel, precision=highest)
    made = (
        rendered.reshape(-1, stamp_size * stamp_size)
        .astype(jnp.bfloat16)
        .reshape(n_sky, capacity, -1)
    )
    stamps = lax.all_to_all(made, "sky", split_axis=0, concat_axis=0, tiled=True).reshape(slots, -1)
    stamps = jnp.where(live_flat, stamps, jnp.zeros_like(stamps))
    block_size = math.gcd(slots, 32)
    blocks = slots // block_size
    stamp_blocks = stamps.reshape(blocks, block_size, stamp_size, stamp_size)
    row_blocks = stamp_row[0].reshape(blocks, block_size)
    col_blocks = stamp_col[0].reshape(blocks, block_size)
    stamp_span = jnp.arange(stamp_size, dtype=jnp.int32)
    lane_index = jnp.arange(width, dtype=jnp.int32)
    level_index = jnp.arange(canvas_rows, dtype=jnp.int32)

    def tables(rows_b, cols_b):
        col_one = (
            cols_b[:, None, None] + stamp_span[None, :, None] == lane_index[None, None, :]
        ).astype(jnp.bfloat16)
        covered = (rows_b[:, None] + stamp_span[None, :]).reshape(1, -1)
        row_one = (level_index[:, None] == covered).astype(jnp.bfloat16)
        return (row_one, col_one)

    def place(canvas, block):
        stamps_b, rows_b, cols_b = block
        row_one, col_one = tables(rows_b, cols_b)
        moved = jnp.einsum(
            "nab,nbj->naj", stamps_b, col_one, preferred_element_type=jnp.float32
        ).astype(jnp.bfloat16)
        return (
            canvas + jnp.dot(row_one, moved.reshape(-1, width), preferred_element_type=jnp.float32),
            None,
        )

    start = jnp.zeros((canvas_rows, width), jnp.float32)
    canvas, unused = lax.scan(place, start, (stamp_blocks, row_blocks, col_blocks))
    margins = jnp.concatenate([canvas[:margin], canvas[margin + tile_rows :]], axis=0)
    spilled = extended_2(margins, (("sky", 0),), margin)
    image = canvas[margin : margin + tile_rows]
    image = (
        image.at[:margin].add(spilled[:margin]).at[tile_rows - margin :].add(spilled[3 * margin :])
    )
    model = background[0] + jax.nn.softplus(image)
    residual = (observed[0] / model - 1.0) * jax.nn.sigmoid(image)
    extended = extended_2(residual.astype(jnp.bfloat16), (("sky", 0),), margin)

    def pick(block):
        rows_b, cols_b = block
        row_one, col_one = tables(rows_b, cols_b)
        lifted = lax.dot_general(
            row_one, extended, (((0,), (0,)), ((), ())), preferred_element_type=jnp.float32
        )
        lifted = lifted.astype(jnp.bfloat16).reshape(block_size, stamp_size, width)
        return jnp.einsum(
            "naj,nbj->nab", lifted, col_one, preferred_element_type=jnp.float32
        ).astype(jnp.bfloat16)

    patches = lax.map(pick, (row_blocks, col_blocks)).reshape(slots, -1)
    patches = jnp.where(live_flat, patches, jnp.zeros_like(patches))
    owned_rows = send_index[0].reshape(-1)
    source_index = jnp.arange(params.shape[0], dtype=jnp.int32)
    scatter_table = (source_index[:, None] == owned_rows[None, :]).astype(jnp.float32)
    returned = lax.all_to_all(
        patches.reshape(n_sky, capacity, -1), "sky", split_axis=0, concat_axis=0, tiled=True
    )
    window = returned.reshape(slots, -1).astype(jnp.float32).reshape(-1, stamp_size, stamp_size)
    pulled = jnp.einsum("ba,nbc,cd->nad", row_kernel, window, col_kernel, precision=highest)
    flat = pulled.reshape(-1, stamp_size * stamp_size)
    slot_grad = jnp.dot(flat, basis_wide, precision=highest).reshape(n_sky, capacity, -1)
    summed = lax.psum(slot_grad, "epoch")
    param_grad = jnp.dot(scatter_table, summed.reshape(slots, -1), precision=highest)
    return (param_grad, residual[None])


def solution(mesh):
    in_specs = (
        P("sky", None),
        P(),
        P("epoch", None, None),
        P("sky", None, None),
        P("sky", None),
        P("sky", None, None),
        P("sky", None, None),
        P("epoch", "sky", None),
        P("epoch", "sky", None),
    )
    out_specs = (P("sky", None), P("epoch", "sky", None))
    return jax.shard_map(
        on_device, mesh=mesh, in_specs=in_specs, out_specs=out_specs, check_vma=False
    )
```

profile of v0, /device:TPU:0, one launch (start us, length us, event | category | flops | bytes accessed | tf_op | source)
XLA Modules:
  0.0 158.2 jit_solution(5530067456147335051)
XLA Ops:
  2.3 24.7 %gather_fusion.1 = f32[4096]{0:T(1024)S(1)} fusion(f32[51]{0:T(128)S(1)} %get-tuple-element.227, s32[4096]{0:T(1024)S(1)} %broadcast_clamp_fusion), kind=kCustom, calls=%fused_computation.1 | custom fusion | bytes 49152 | tf_op jit(solution)/shard_map/gather | solution.py:33
  28.5 24.7 %gather_fusion.2 = f32[4096]{0:T(1024)S(1)} fusion(f32[51]{0:T(128)S(1)} %get-tuple-element.226, s32[4096]{0:T(1024)S(1)} %broadcast_clamp_fusion), kind=kCustom, calls=%fused_computation.2 | custom fusion | bytes 49152 | tf_op jit(solution)/shard_map/gather | solution.py:33
  54.8 3.3 %fusion.31 = f32[64,64,64]{1,2,0:T(8,128)S(1)} fusion(f32[64,64,64]{2,0,1:T(8,128)S(1)} %fusion.33, f32[64,64]{1,0:T(8,128)S(1)} %reshape.307), kind=kOutput, calls=%fused_computation.41 | convolution fusion | flops 201351168 | bytes 2113536 | tf_op jit(solution)/shard_map/ab,nbc,dc->nad/dot_general | solution.py:58
  58.1 1.8 %convolution_convert_fusion.1 = bf16[64,64,64]{2,1,0:T(8,128)(2,1)S(1)} fusion(f32[64,64,64]{1,2,0:T(8,128)S(1)} %fusion.31, f32[64,64]{1,0:T(8,128)S(1)} %reshape.315), kind=kOutput, calls=%fused_computation.44 | convolution fusion | flops 201613312 | bytes 1589248 | tf_op jit(solution)/shard_map/ab,nbc,dc->nad/dot_general | solution.py:58
  59.9 1.6 %convert_element_type.27 = bf16[4,16,4096]{2,1,0:T(8,128)(2,1)} reshape(bf16[64,64,64]{2,1,0:T(8,128)(2,1)S(1)} %convolution_convert_fusion.1) | data formatting | bytes 1048576 | tf_op jit(solution)/shard_map/convert_element_type | solution.py:61
  61.5 5.2 %all-to-all-start = ((bf16[4,16,4096]{2,1,0:T(8,128)(2,1)}), bf16[4,16,4096]{2,1,0:T(8,128)(2,1)S(1)}, u32[]{:S(2)}, u32[]{:S(2)}) async-start(bf16[4,16,4096]{2,1,0:T(8,128)(2,1)} %convert_element_type.27), calls=%async_computation | async-start | bytes 1048576 | tf_op jit(solution)/shard_map/all_to_all | solution.py:64
  68.5 6.2 %all-to-all-done = bf16[4,16,4096]{2,1,0:T(8,128)(2,1)S(1)} async-done(((bf16[4,16,4096]{2,1,0:T(8,128)(2,1)}), bf16[4,16,4096]{2,1,0:T(8,128)(2,1)S(1)}, u32[]{:S(2)}, u32[]{:S(2)}) %all-to-all-start) | async-done | bytes 524320 | tf_op jit(solution)/shard_map/all_to_all | solution.py:64
  76.0 7.4 %while.29 = (s32[]{:T(128)}, f32[320,512]{1,0:T(8,128)}, s32[2,32]{1,0:T(2,128)S(1)}, bf16[2,32,64,64]{3,2,1,0:T(8,128)(2,1)S(1)}, s32[2,32]{1,0:T(2,128)S(1)}) while((s32[]{:T(128)}, f32[320,512]{1,0:T(8,128)}, s32[2,32]{1,0:T(2,128)S(1)}, bf16[2,32,64,64]{3,2,1,0:T(8,128)(2,1)S(1)}, ...), condition=%wide.region_2.3_spmd.clone.clone.clone, body=%wide.region_1.2_spmd.clone.clone.sunk.clone | while | flops 808390656 | bytes 6087503 | solution.py:95
  77.4 1.7 %fusion.120 = f32[320,512]{1,0:T(8,128)} fusion(bf16[2048,512]{1,0:T(8,128)(2,1)S(1)} %bitcast.94, s32[2048]{0:T(1024)S(1)} %add.305, f32[320,512]{1,0:T(8,128)} %get-tuple-element.333, pred[]{:T(512)S(6)} %compare.14), kind=kOutput, calls=%fused_computation.31.clone.1.clone | convolution fusion | flops 672071680 | bytes 3416065 | tf_op jit(solution)/shard_map/while/body/eval_jaxpr/dot_general | solution.py:90
  80.5 2.8 %fusion.120 = f32[320,512]{1,0:T(8,128)} fusion(bf16[2048,512]{1,0:T(8,128)(2,1)S(1)} %bitcast.94, s32[2048]{0:T(1024)S(1)} %add.305, f32[320,512]{1,0:T(8,128)} %get-tuple-element.333, pred[]{:T(512)S(6)} %compare.14), kind=kOutput, calls=%fused_computation.31.clone.1.clone | convolution fusion | flops 672071680 | bytes 3416065 | tf_op jit(solution)/shard_map/while/body/eval_jaxpr/dot_general | solution.py:90
  84.2 3.3 %collective-permute-start = (f32[32,512]{1,0:T(8,128)S(1)}, f32[32,512]{1,0:T(8,128)S(1)}, u32[]{:S(2)}, u32[]{:S(2)}) collective-permute-start(f32[32,512]{1,0:T(8,128)S(1)} %get-tuple-element.223), channel_id=1, source_target_pairs={{0,8},{8,16},{16,24},{1,9},{9,17},{17,25},{2,10},{10,18},{18,26},{... | collective-permute-start | bytes 196616 | tf_op jit(solution)/shard_map/ppermute | solution.py:17
  88.6 1.3 collective-permute-start.1
  90.8 4.0 %collective-permute-done.1 = f32[32,512]{1,0:T(8,128)S(1)} collective-permute-done((f32[32,512]{1,0:T(8,128)S(1)}, f32[32,512]{1,0:T(8,128)S(1)}, u32[]{:S(2)}, u32[]{:S(2)}) %collective-permute-start.1) | collective-permute-done | bytes 65568 | tf_op jit(solution)/shard_map/ppermute | solution.py:19
  94.8 2.4 %fusion.82 = (bf16[256,512]{1,0:T(8,128)(2,1)S(1)}, f32[256,512]{1,0:T(8,128)}) fusion(f32[256,512]{1,0:T(8,128)S(1)} %fusion.41, f32[1,256,512]{2,1,0:T(8,128)} %param.25, f32[1,256,512]{2,1,0:T(8,128)} %param.24), kind=kLoop, calls=%fused_computation.105 | loop fusion | flops 1835008 | bytes 2359296 | tf_op jit(solution)/shard_map/convert_element_type | solution.py:104
  97.3 4.5 %collective-permute-start.2 = (bf16[32,512]{1,0:T(8,128)(2,1)S(1)}, bf16[32,512]{1,0:T(8,128)(2,1)S(1)}, u32[]{:S(2)}, u32[]{:S(2)}) collective-permute-start(bf16[32,512]{1,0:T(8,128)(2,1)S(1)} %get-tuple-element.224), channel_id=1, source_target_pairs={{0,8},{8,16},{16,24},{1,9},{9,17},{17,25},{2,10},{10,18},{18,26},{... | collective-permute-start | bytes 98312 | tf_op jit(solution)/shard_map/ppermute | solution.py:17
  103.3 4.2 %collective-permute-done.3 = bf16[32,512]{1,0:T(8,128)(2,1)S(1)} collective-permute-done((bf16[32,512]{1,0:T(8,128)(2,1)S(1)}, bf16[32,512]{1,0:T(8,128)(2,1)S(1)}, u32[]{:S(2)}, u32[]{:S(2)}) %collective-permute-start.3) | collective-permute-done | bytes 32800 | tf_op jit(solution)/shard_map/ppermute | solution.py:19
  107.6 5.7 %while.28 = (s32[]{:T(128)}, bf16[2,32,64,64]{3,2,1,0:T(8,128)(2,1)S(1)}, s32[2,32]{1,0:T(2,128)S(1)}, bf16[320,512]{1,0:T(8,128)(2,1)S(1)}, s32[2,32]{1,0:T(2,128)S(1)}) while((s32[]{:T(128)}, bf16[2,32,64,64]{3,2,1,0:T(8,128)(2,1)S(1)}, s32[2,32]{1,0:T(2,128)S(1)}, bf16[320,512]{1,0:T(8,128)(2,1)S(1)}, ...), condition=%wide.region_4.5_spmd.clone.clone.clone, body=%wide.region_3.4_spmd.clone.clone.sunk.clone | while | flops 808194048 | bytes 5104453 | solution.py:117
  107.8 1.3 convolution_convert_fusion.4
  110.6 1.3 convolution_convert_fusion.4
  115.0 3.5 %all-to-all-start.1 = ((bf16[4,16,4096]{2,1,0:T(8,128)(2,1)}), bf16[4,16,4096]{2,1,0:T(8,128)(2,1)S(1)}, u32[]{:S(2)}, u32[]{:S(2)}) async-start(bf16[4,16,4096]{2,1,0:T(8,128)(2,1)} %broadcast_select_fusion.1), calls=%async_computation.1 | async-start | bytes 1048576 | tf_op jit(solution)/shard_map/all_to_all | solution.py:122
  118.6 6.5 %all-to-all-done.1 = bf16[4,16,4096]{2,1,0:T(8,128)(2,1)S(1)} async-done(((bf16[4,16,4096]{2,1,0:T(8,128)(2,1)}), bf16[4,16,4096]{2,1,0:T(8,128)(2,1)S(1)}, u32[]{:S(2)}, u32[]{:S(2)}) %all-to-all-start.1) | async-done | bytes 524320 | tf_op jit(solution)/shard_map/all_to_all | solution.py:122
  127.2 1.8 %fusion.43 = f32[64,64,64]{2,1,0:T(8,128)S(1)} fusion(f32[64,64,64]{1,2,0:T(8,128)S(1)} %fusion.46, f32[64,64]{1,0:T(8,128)S(1)} %reshape.315), kind=kOutput, calls=%fused_computation.62 | convolution fusion | flops 201351168 | bytes 2113536 | tf_op jit(solution)/shard_map/ba,nbc,cd->nad/dot_general | solution.py:126
  129.7 1.7 %fusion.39 = f32[4,16,64]{2,1,0:T(8,128)S(1)} fusion(f32[4,16,4096]{2,1,0:T(8,128)S(1)} %dot_general.46, bf16[64,4096]{1,0:T(8,128)(2,1)} %param.18), kind=kOutput, calls=%fused_computation.52 | convolution fusion | flops 201326592 | bytes 1589248 | tf_op jit(solution)/shard_map/dot_general | solution.py:128
  131.3 26.0 %psum.7 = f32[64,64]{1,0:T(8,128)S(1)} all-reduce(f32[64,64]{1,0:T(8,128)S(1)} %bitcast.97), channel_id=1, replica_groups=mesh['sky'=4,'epoch'=8] {'epoch'}, use_global_device_ids=true, to_apply=%region_5.6 | all-reduce | flops 4096 | bytes 32768 | tf_op jit(solution)/shard_map/psum | solution.py:129
  (78 shorter events, 23.5 us)
Async XLA Ops:
  2.3 24.8 %copy-start = (bf16[64,4096]{1,0:T(8,128)(2,1)S(1)}, bf16[64,4096]{1,0:T(8,128)(2,1)}, u32[]{:S(2)}) copy-start(bf16[64,4096]{1,0:T(8,128)(2,1)} %param.18) | copy-start | bytes 1572868
  2.3 25.9 %copy-start.1 = (bf16[128,64]{0,1:T(8,128)(2,1)S(1)}, bf16[128,64]{0,1:T(8,128)(2,1)}, u32[]{:S(2)}) copy-start(bf16[128,64]{0,1:T(8,128)(2,1)} %param.17) | copy-start | bytes 49156
  2.3 26.1 %copy-start.2 = (s32[1,4,16]{2,1,0:T(4,128)S(1)}, s32[1,4,16]{2,1,0:T(4,128)}, u32[]{:S(2)}) copy-start(s32[1,4,16]{2,1,0:T(4,128)} %param.20) | copy-start | bytes 772
  59.9 7.4 %copy-start.5 = (s32[1,4]{1,0:T(1,128)S(1)}, s32[1,4]{1,0:T(1,128)}, u32[]{:S(2)}) copy-start(s32[1,4]{1,0:T(1,128)} %param.21) | copy-start | bytes 52
  59.9 8.4 %copy-start.3 = (s32[1,4,16]{2,1,0:T(4,128)S(1)}, s32[1,4,16]{2,1,0:T(4,128)}, u32[]{:S(2)}) copy-start(s32[1,4,16]{2,1,0:T(4,128)} %param.22) | copy-start | bytes 772
  59.9 8.5 %copy-start.4 = (s32[1,4,16]{2,1,0:T(4,128)S(1)}, s32[1,4,16]{2,1,0:T(4,128)}, u32[]{:S(2)}) copy-start(s32[1,4,16]{2,1,0:T(4,128)} %param.23) | copy-start | bytes 772
  61.5 13.2 %all-to-all-start = ((bf16[4,16,4096]{2,1,0:T(8,128)(2,1)}), bf16[4,16,4096]{2,1,0:T(8,128)(2,1)S(1)}, u32[]{:S(2)}, u32[]{:S(2)}) async-start(bf16[4,16,4096]{2,1,0:T(8,128)(2,1)} %convert_element_type.27), calls=%async_computation | async-start | bytes 1048576 | tf_op jit(solution)/shard_map/all_to_all | solution.py:64
  84.2 5.7 %collective-permute-start = (f32[32,512]{1,0:T(8,128)S(1)}, f32[32,512]{1,0:T(8,128)S(1)}, u32[]{:S(2)}, u32[]{:S(2)}) collective-permute-start(f32[32,512]{1,0:T(8,128)S(1)} %get-tuple-element.223), channel_id=1, source_target_pairs={{0,8},{8,16},{16,24},{1,9},{9,17},{17,25},{2,10},{10,18},{18,26},{... | collective-permute-start | bytes 196616 | tf_op jit(solution)/shard_map/ppermute | solution.py:17
  88.6 6.2 %collective-permute-start.1 = (f32[32,512]{1,0:T(8,128)S(1)}, f32[32,512]{1,0:T(8,128)S(1)}, u32[]{:S(2)}, u32[]{:S(2)}) collective-permute-start(f32[32,512]{1,0:T(8,128)S(1)} %get-tuple-element.222), channel_id=1, source_target_pairs={{8,0},{16,8},{24,16},{9,1},{17,9},{25,17},{10,2},{18,10},{26,18},{... | collective-permute-start | bytes 196616 | tf_op jit(solution)/shard_map/ppermute | solution.py:19
  97.3 6.1 %collective-permute-start.2 = (bf16[32,512]{1,0:T(8,128)(2,1)S(1)}, bf16[32,512]{1,0:T(8,128)(2,1)S(1)}, u32[]{:S(2)}, u32[]{:S(2)}) collective-permute-start(bf16[32,512]{1,0:T(8,128)(2,1)S(1)} %get-tuple-element.224), channel_id=1, source_target_pairs={{0,8},{8,16},{16,24},{1,9},{9,17},{17,25},{2,10},{10,18},{18,26},{... | collective-permute-start | bytes 98312 | tf_op jit(solution)/shard_map/ppermute | solution.py:17
  101.8 5.8 %collective-permute-start.3 = (bf16[32,512]{1,0:T(8,128)(2,1)S(1)}, bf16[32,512]{1,0:T(8,128)(2,1)S(1)}, u32[]{:S(2)}, u32[]{:S(2)}) collective-permute-start(bf16[32,512]{1,0:T(8,128)(2,1)S(1)} %get-tuple-element.225), channel_id=1, source_target_pairs={{8,0},{16,8},{24,16},{9,1},{17,9},{25,17},{10,2},{18,10},{26,18},{... | collective-permute-start | bytes 98312 | tf_op jit(solution)/shard_map/ppermute | solution.py:19
  115.0 10.0 %all-to-all-start.1 = ((bf16[4,16,4096]{2,1,0:T(8,128)(2,1)}), bf16[4,16,4096]{2,1,0:T(8,128)(2,1)S(1)}, u32[]{:S(2)}, u32[]{:S(2)}) async-start(bf16[4,16,4096]{2,1,0:T(8,128)(2,1)} %broadcast_select_fusion.1), calls=%async_computation.1 | async-start | bytes 1048576 | tf_op jit(solution)/shard_map/all_to_all | solution.py:122
where the time goes:
time: 159 us; the launch traced here: 158 us
  local copies, waits for them, and re-layouts  60.4 us (38%)
  blocking collectives  26 us (16%)
  matrix products  23.4 us (15%)
  waiting for transfers between devices  21.1 us (13%)
  starting transfers between devices  19 us (12%)
  other arithmetic  7.31 us (5%)
    gather x4, local copies, waits for them, and re-layouts, toeplitz(): taps[jnp.clip(where_at, 0, taps.shape[0] - 1)]  49.5 us
    psum x1, blocking collectives, on_device(): summed = lax.psum(slot_grad, 'epoch')  26 us
    ppermute x2, waiting for transfers between devices, extended_2(): lax.ppermute(head, axis, [((i + 1) % count, i) for i in range(ends)])  8.22 us
    ppermute x2, starting transfers between devices, extended_2(): lax.ppermute(tail, axis, [(i, (i + 1) % count) for i in range(ends)])  7.81 us
    all_to_all x1, waiting for transfers between devices, on_device(): lax.all_to_all(patches.reshape(n_sky, capacity, -1), 'sky', split_axis=0,...  6.46 us
    all_to_all x1, waiting for transfers between devices, on_device(): lax.all_to_all(made, 'sky', split_axis=0, concat_axis=0, tiled=True)  6.23 us
    all_to_all x1, starting transfers between devices, on_device(): lax.all_to_all(made, 'sky', split_axis=0, concat_axis=0, tiled=True)  5.17 us
    dot_general x2, matrix products, on_device(): jnp.einsum('ab,nbc,dc->nad', row_kernel, intrinsic, col_kernel, precision...  5.07 us
  transfers between devices with their start and end apart: 6, of which 5 were waited for; matrix products, arithmetic and copies ran while one was open for 2% of the time, Pallas kernels for 0%

commit v1 on v0

v1 whole, which is shorter than its diff:
```python
import functools

import jax
import jax.numpy as jnp
from jax import lax
from jax.experimental import pallas as pl
from jax.experimental.pallas import tpu as pltpu
from jax.sharding import PartitionSpec as P

MESH = pl.DeviceIdType.MESH
LANES = 128


def split_two(value):
    high = value.astype(jnp.bfloat16)
    return high, (value - high.astype(jnp.float32)).astype(jnp.bfloat16)


def wide_dot(left, right, dims=(((1,), (0,)), ((), ()))):
    return lax.dot_general(left, right, dims, preferred_element_type=jnp.float32)


def kernel(
    n_sky,
    n_epoch,
    params,
    basis,
    taps_scalar,
    taps_vector,
    send_index,
    tile_count,
    stamp_row,
    stamp_col,
    observed,
    background,
    grad_out,
    residual_out,
    outgoing,
    incoming,
    observed_halo,
    background_halo,
    basis_rows,
    basis_mixed,
    rendered_rows,
    rendered,
    stamps,
    row_one,
    moved,
    canvas,
    light_halo,
    reach,
    window_rows,
    windows,
    slot_grad,
    reduce_in,
    piece,
    gather_in,
    param_send,
    param_recv,
    halo_send,
    halo_recv,
    light_send,
    light_recv,
    reduce_send,
    reduce_recv,
    gather_send,
    gather_recv,
):
    me_s = lax.axis_index("sky")
    me_e = lax.axis_index("epoch")
    n_par = params.shape[1]
    size = 64
    half = size // 2
    capacity = send_index.shape[2]
    slots = n_sky * capacity
    tile_rows = observed.shape[1]
    width = observed.shape[2]
    margin = half
    canvas_rows = tile_rows + 2 * margin
    planes = width // LANES
    pairs = size * size // LANES
    per = slots // n_epoch
    ratio = capacity // per
    n_taps = taps_vector.shape[2]
    reach_taps = (n_taps - 1) // 2
    my_owner = me_e // ratio
    has_above = me_s > 0
    has_below = me_s < n_sky - 1

    barrier = pltpu.get_barrier_semaphore()
    for step in range(1, n_sky):
        pl.semaphore_signal(
            barrier, 1, device_id=(lax.rem(me_s + step, n_sky), me_e), device_id_type=MESH
        )
    for step in range(1, n_epoch):
        pl.semaphore_signal(
            barrier, 1, device_id=(me_s, lax.rem(me_e + step, n_epoch)), device_id_type=MESH
        )
    for tile in range(n_sky):
        for part in range(ratio):
            sender = me_s * ratio + part

            @pl.when(jnp.logical_not((me_s == tile) & (sender == me_e)))
            def _():
                pl.semaphore_signal(barrier, 1, device_id=(tile, sender), device_id_type=MESH)

    slot_at = lax.broadcasted_iota(jnp.int32, (slots, params.shape[0]), 0)
    source_at = lax.broadcasted_iota(jnp.int32, (slots, params.shape[0]), 1)
    named = jnp.zeros_like(slot_at)
    for tile in range(n_sky):
        for k in range(capacity):
            named = jnp.where(slot_at == tile * capacity + k, send_index[0, tile, k], named)
    picked = wide_dot((named == source_at).astype(jnp.bfloat16), params[...]).astype(jnp.bfloat16)
    for tile in range(n_sky):
        outgoing[tile] = picked[tile * capacity : (tile + 1) * capacity]
    incoming[me_s] = outgoing[me_s]

    pl.semaphore_wait(
        barrier,
        (n_sky - 1) + (n_epoch - 1) + n_epoch - jnp.where(my_owner == me_s, 1, 0),
    )

    def param_copy(step):
        other = lax.rem(me_s + step, n_sky)
        return pltpu.make_async_remote_copy(
            src_ref=outgoing.at[other],
            dst_ref=incoming.at[me_s],
            send_sem=param_send.at[step],
            recv_sem=param_recv.at[step],
            device_id=(other, me_e),
            device_id_type=MESH,
        )

    def halo_copies(upward):
        other = me_s - 1 if upward else me_s + 1
        start = 0 if upward else tile_rows - margin
        slot = 1 if upward else 0
        return [
            pltpu.make_async_remote_copy(
                src_ref=array.at[0, pl.ds(start, margin)],
                dst_ref=landing.at[slot],
                send_sem=halo_send.at[which, slot],
                recv_sem=halo_recv.at[which, slot],
                device_id=(other, me_e),
                device_id_type=MESH,
            )
            for which, (array, landing) in enumerate(
                ((observed, observed_halo), (background, background_halo))
            )
        ]

    def light_copy(upward):
        other = me_s - 1 if upward else me_s + 1
        start = 0 if upward else canvas_rows - 2 * margin
        slot = 1 if upward else 0
        return pltpu.make_async_remote_copy(
            src_ref=canvas.at[pl.ds(start, 2 * margin)],
            dst_ref=light_halo.at[slot],
            send_sem=light_send.at[slot],
            recv_sem=light_recv.at[slot],
            device_id=(other, me_e),
            device_id_type=MESH,
        )

    for step in range(1, n_sky):
        param_copy(step).start()

    @pl.when(has_above)
    def _():
        for copy in halo_copies(True):
            copy.start()

    @pl.when(has_below)
    def _():
        for copy in halo_copies(False):
            copy.start()

    @pl.when(jnp.logical_not(has_above))
    def _():
        light_halo[0] = jnp.zeros(light_halo.shape[1:], jnp.float32)
        observed_halo[0] = jnp.zeros(observed_halo.shape[1:], jnp.float32)
        background_halo[0] = jnp.ones(background_halo.shape[1:], jnp.float32)

    @pl.when(jnp.logical_not(has_below))
    def _():
        light_halo[1] = jnp.zeros(light_halo.shape[1:], jnp.float32)
        observed_halo[1] = jnp.zeros(observed_halo.shape[1:], jnp.float32)
        background_halo[1] = jnp.ones(background_halo.shape[1:], jnp.float32)

    def natural(value):
        return 2 * (value % half) + value // half

    row_a = natural(lax.broadcasted_iota(jnp.int32, (size, size), 0))
    row_b = natural(lax.broadcasted_iota(jnp.int32, (size, size), 1))
    row_where = row_a - row_b + reach_taps
    col_c = lax.broadcasted_iota(jnp.int32, (LANES, LANES), 0)
    col_d = lax.broadcasted_iota(jnp.int32, (LANES, LANES), 1)
    col_where = jnp.where(
        col_c // size == col_d // size, col_d % size - col_c % size + reach_taps, -1
    )

    def tap_step(tap, both):
        row_k, col_k = both
        return (
            jnp.where(row_where == tap, taps_scalar[0, 0, tap], row_k),
            jnp.where(col_where == tap, taps_scalar[0, 1, tap], col_k),
        )

    row_k, col_k = lax.fori_loop(
        0,
        n_taps,
        tap_step,
        (jnp.zeros((size, size), jnp.float32), jnp.zeros((LANES, LANES), jnp.float32)),
        unroll=3,
    )
    total = jnp.sum(taps_vector[0], axis=1, keepdims=True)
    row_high, row_low = split_two(row_k / total[0:1])
    col_high, col_low = split_two(col_k / total[1:2])

    lane_half = lax.broadcasted_iota(jnp.int32, (half, LANES), 1) < size
    for pair in range(pairs):
        basis_rows[pl.ds(pair * n_par, n_par), :] = basis[
            :, pair * LANES : (pair + 1) * LANES
        ].astype(jnp.float32)

    def swapped(one, two):
        return (
            jnp.where(lane_half, one, pltpu.roll(two, size, 1)),
            jnp.where(lane_half, pltpu.roll(one, size, 1), two),
        )

    group = 8

    def mix_group(index, carry):
        for inner in range(group):
            pp = index * group + inner
            one = basis_rows[pl.ds(2 * pp, half, stride=n_par), :]
            two = basis_rows[pl.ds(2 * pp + 1, half, stride=n_par), :]
            first, second = swapped(one, two)
            lanes = pl.ds(inner * LANES, LANES)
            basis_mixed[:half, lanes] = first.astype(jnp.bfloat16)
            basis_mixed[half:, lanes] = second.astype(jnp.bfloat16)
        mixed = basis_mixed[...]
        by_row = wide_dot(row_high, mixed) + wide_dot(row_low, mixed)
        tall = jnp.concatenate(
            [by_row[:, inner * LANES : (inner + 1) * LANES] for inner in range(group)], axis=0
        )
        high, low = split_two(tall)
        done = wide_dot(high, col_high) + (wide_dot(low, col_high) + wide_dot(high, col_low))
        for inner in range(group):
            pp = index * group + inner
            base = inner * size
            first, second = swapped(done[base : base + half], done[base + half : base + size])
            rendered_rows[pl.ds(2 * pp, half, stride=n_par), :] = first
            rendered_rows[pl.ds(2 * pp + 1, half, stride=n_par), :] = second
        return carry

    lax.fori_loop(0, n_par // 2 // group, mix_group, 0)
    for pair in range(pairs):
        high, low = split_two(rendered_rows[pl.ds(pair * n_par, n_par), :])
        rendered[:n_par, pair * LANES : (pair + 1) * LANES] = high
        rendered[n_par:, pair * LANES : (pair + 1) * LANES] = low

    for step in range(1, n_sky):
        copy = param_copy(step)
        copy.wait()
    par_slot = lax.broadcasted_iota(jnp.int32, (slots, n_par), 0)
    live = jnp.zeros((slots, n_par), jnp.float32)
    for owner in range(n_sky):
        inside = (par_slot >= owner * capacity) & (
            par_slot < owner * capacity + tile_count[0, owner]
        )
        live = jnp.where(inside & (par_slot < (owner + 1) * capacity), 1.0, live)
    here = incoming[...].reshape(slots, n_par).astype(jnp.float32)
    here = jnp.where(live > 0, here, 0.0).astype(jnp.bfloat16)
    wide = 8
    for block in range(pairs // wide):
        lanes = slice(block * wide * LANES, (block + 1) * wide * LANES)
        made = wide_dot(here, rendered[:n_par, lanes]) + wide_dot(here, rendered[n_par:, lanes])
        for inner in range(wide):
            stamps[pl.ds((block * wide + inner) * slots, slots), :] = made[
                :, inner * LANES : (inner + 1) * LANES
            ]

    lane_row = lax.broadcasted_iota(jnp.int32, (1, LANES), 1)
    level = lax.broadcasted_iota(jnp.int32, (canvas_rows, LANES), 0)
    offset = level - natural(lax.broadcasted_iota(jnp.int32, (canvas_rows, LANES), 1) % size)
    canvas[...] = jnp.zeros_like(canvas)

    def place_owner(owner, carry):
        def place_pair(pair, inner_carry):
            rows = []
            for which in range(2):
                k = 2 * pair + which
                col = stamp_col[0, owner, k]
                rows.append(stamp_row[0, owner, k])
                stamp = stamps[pl.ds(owner * capacity + k, half, stride=slots), :]
                shift = lax.rem(col, LANES)
                even = pltpu.roll(stamp, shift, 1)
                odd = pltpu.roll(even, size, 1)
                for plane in range(planes):
                    at = lane_row + (plane * LANES) - col
                    inside = (at >= 0) & (at < size)
                    for parity, data in enumerate((even, odd)):
                        start = pl.multiple_of(k * size + parity * half, half)
                        moved[pl.ds(start, half), plane * LANES : (plane + 1) * LANES] = jnp.where(
                            inside, data, 0.0
                        ).astype(jnp.bfloat16)
            target = jnp.where(lane_row < size, rows[0], rows[1])
            lanes = pl.ds(pl.multiple_of(pair * LANES, LANES), LANES)
            row_one[:, lanes] = jnp.where(offset == target, 1.0, 0.0).astype(jnp.bfloat16)
            return inner_carry

        lax.fori_loop(0, capacity // 2, place_pair, 0, unroll=2)
        canvas[...] += wide_dot(row_one[...], moved[...])
        return carry

    lax.fori_loop(0, n_sky, place_owner, 0)

    @pl.when(has_above)
    def _():
        light_copy(True).start()

    @pl.when(has_below)
    def _():
        light_copy(False).start()

    def residual_of(image, seen, sky):
        decay = jnp.exp(-jnp.abs(image))
        model = sky + (jnp.maximum(image, 0.0) + jnp.log(1.0 + decay))
        numerator = jnp.where(image >= 0, 1.0, decay)
        return (seen - model) * numerator / (model * (1.0 + decay))

    def keep(value, start):
        rounded = value.astype(jnp.bfloat16).astype(jnp.float32)
        for plane in range(planes):
            reach[pl.ds(plane * canvas_rows + start, margin), :] = rounded[
                :, plane * LANES : (plane + 1) * LANES
            ]

    def core_chunk(index, carry):
        start = pl.multiple_of(index * margin, margin)
        inner = pl.multiple_of(start - margin, margin)
        value = residual_of(
            canvas[pl.ds(start, margin), :],
            observed[0, pl.ds(inner, margin), :],
            background[0, pl.ds(inner, margin), :],
        )
        residual_out[0, pl.ds(inner, margin), :] = value
        keep(value, start)
        return carry

    chunks = canvas_rows // margin
    lax.fori_loop(2, chunks - 2, core_chunk, 0)
    reach[planes * canvas_rows :, :] = jnp.zeros((canvas_rows, LANES), jnp.float32)

    @pl.when(has_above)
    def _():
        light_copy(True).wait_send()
        light_copy(False).wait_recv()
        for copy in halo_copies(True):
            copy.wait_send()
        for copy in halo_copies(False):
            copy.wait_recv()

    @pl.when(has_below)
    def _():
        light_copy(False).wait_send()
        light_copy(True).wait_recv()
        for copy in halo_copies(False):
            copy.wait_send()
        for copy in halo_copies(True):
            copy.wait_recv()

    for slot, exists in ((0, has_above), (1, has_below)):
        outer = 0 if slot == 0 else canvas_rows - margin
        inner = margin if slot == 0 else canvas_rows - 2 * margin
        outer_light = 0 if slot == 0 else margin
        inner_light = margin - outer_light
        value = residual_of(
            canvas[pl.ds(outer, margin), :] + light_halo[slot, pl.ds(outer_light, margin), :],
            observed_halo[slot],
            background_halo[slot],
        )
        keep(jnp.where(exists, value, 0.0), outer)
        value = residual_of(
            canvas[pl.ds(inner, margin), :] + light_halo[slot, pl.ds(inner_light, margin), :],
            observed[0, pl.ds(inner - margin, margin), :],
            background[0, pl.ds(inner - margin, margin), :],
        )
        residual_out[0, pl.ds(inner - margin, margin), :] = value
        keep(value, inner)

    def pick_owner(owner, carry):
        def pick(k, inner_carry):
            col = stamp_col[0, owner, k]
            row = stamp_row[0, owner, k]
            shift = lax.rem(col, LANES)
            first = (col // LANES) * canvas_rows + row
            back = lax.rem(LANES - shift, LANES)
            halves = []
            for parity in range(2):
                near = reach[pl.ds(first + parity, half, stride=2), :]
                far = reach[pl.ds(first + canvas_rows + parity, half, stride=2), :]
                halves.append(jnp.where(lane_row >= shift, near, far))
            even = pltpu.roll(halves[0], back, 1)
            odd = pltpu.roll(pltpu.roll(halves[1], back, 1), size, 1)
            window_rows[pl.ds(owner * capacity + k, half, stride=slots), :] = jnp.where(
                lane_half, even, odd
            )
            return inner_carry

        return lax.fori_loop(0, capacity, pick, carry, unroll=4)

    lax.fori_loop(0, n_sky, pick_owner, 0)
    for pair in range(pairs):
        windows[:, pair * LANES : (pair + 1) * LANES] = window_rows[
            pl.ds(pair * slots, slots), :
        ].astype(jnp.bfloat16)
    both = wide_dot(windows[...], rendered[...], (((1,), (1,)), ((), ())))
    slot_grad[...] = jnp.where(live > 0, both[:, :n_par] + both[:, n_par:], 0.0)

    def reduce_copy(step):
        other = lax.rem(me_e + step, n_epoch)
        return pltpu.make_async_remote_copy(
            src_ref=slot_grad.at[pl.ds(pl.multiple_of(other * per, per), per)],
            dst_ref=reduce_in.at[step],
            send_sem=reduce_send.at[step],
            recv_sem=reduce_recv.at[step],
            device_id=(me_s, other),
            device_id_type=MESH,
        )

    for step in range(1, n_epoch):
        reduce_copy(step).start()
    summed = slot_grad[pl.ds(pl.multiple_of(me_e * per, per), per), :]
    for step in range(1, n_epoch):
        reduce_copy(step).wait_recv()
        summed = summed + reduce_in[step]
    piece[...] = summed
    my_place = me_s * ratio + lax.rem(me_e, ratio)

    def gather_copy(step):
        return pltpu.make_async_remote_copy(
            src_ref=piece,
            dst_ref=gather_in.at[my_place],
            send_sem=gather_send.at[step],
            recv_sem=gather_recv.at[my_place],
            device_id=(my_owner, lax.rem(me_e + step, n_epoch)),
            device_id_type=MESH,
        )

    for step in range(1, n_epoch):
        gather_copy(step).start()

    @pl.when(my_owner == me_s)
    def _():
        gather_in[my_place] = piece[...]

    @pl.when(my_owner != me_s)
    def _():
        gather_copy(0).start()

    out_source = lax.broadcasted_iota(jnp.int32, (params.shape[0], slots), 0)
    out_slot = lax.broadcasted_iota(jnp.int32, (1, slots), 1)
    out_named = jnp.zeros((1, slots), jnp.int32)
    for tile in range(n_sky):
        for k in range(capacity):
            out_named = jnp.where(
                out_slot == tile * capacity + k, send_index[0, tile, k], out_named
            )
    table = (out_source == out_named).astype(jnp.float32)

    for step in range(1, n_epoch):
        reduce_copy(step).wait_send()
        gather_copy(step).wait_send()

    @pl.when(my_owner != me_s)
    def _():
        gather_copy(0).wait_send()

    for tile in range(n_sky):
        for part in range(ratio):

            @pl.when(jnp.logical_not((me_s == tile) & (me_s * ratio + part == me_e)))
            def _():
                place = tile * ratio + part
                pltpu.make_async_remote_copy(
                    src_ref=piece,
                    dst_ref=gather_in.at[place],
                    send_sem=gather_send.at[0],
                    recv_sem=gather_recv.at[place],
                    device_id=(tile, me_s * ratio + part),
                    device_id_type=MESH,
                ).wait_recv()

    back = gather_in[...].reshape(slots, n_par)
    grad_out[...] = lax.dot_general(
        table,
        back,
        (((1,), (0,)), ((), ())),
        precision=lax.Precision.HIGHEST,
        preferred_element_type=jnp.float32,
    )


def on_device(
    n_sky,
    n_epoch,
    params,
    basis,
    psf_taps,
    send_index,
    tile_count,
    stamp_row,
    stamp_col,
    observed,
    background,
):
    n_par, pixels = basis.shape
    capacity = send_index.shape[2]
    slots = n_sky * capacity
    tile_rows, width = observed.shape[1:]
    size = 64
    margin = size // 2
    canvas_rows = tile_rows + 2 * margin
    planes = width // LANES
    pairs = pixels // LANES
    per = slots // n_epoch
    ratio = capacity // per
    f32, bf16 = jnp.float32, jnp.bfloat16
    vmem = pl.BlockSpec(memory_space=pltpu.VMEM)
    smem = pl.BlockSpec(memory_space=pltpu.SMEM)
    dma = pltpu.SemaphoreType.DMA
    return pl.pallas_call(
        functools.partial(kernel, n_sky, n_epoch),
        out_shape=(
            jax.ShapeDtypeStruct((params.shape[0], n_par), f32),
            jax.ShapeDtypeStruct(observed.shape, f32),
        ),
        in_specs=[vmem, vmem, smem, vmem, smem, smem, smem, smem, vmem, vmem],
        out_specs=(vmem, vmem),
        scratch_shapes=[
            pltpu.VMEM((n_sky, capacity, n_par), bf16),
            pltpu.VMEM((n_sky, capacity, n_par), bf16),
            pltpu.VMEM((2, margin, width), f32),
            pltpu.VMEM((2, margin, width), f32),
            pltpu.VMEM((pairs * n_par, LANES), f32),
            pltpu.VMEM((size, 8 * LANES), bf16),
            pltpu.VMEM((pairs * n_par, LANES), f32),
            pltpu.VMEM((2 * n_par, pixels), bf16),
            pltpu.VMEM((pairs * slots, LANES), f32),
            pltpu.VMEM((canvas_rows, capacity * size), bf16),
            pltpu.VMEM((capacity * size, width), bf16),
            pltpu.VMEM((canvas_rows, width), f32),
            pltpu.VMEM((2, 2 * margin, width), f32),
            pltpu.VMEM(((planes + 1) * canvas_rows, LANES), f32),
            pltpu.VMEM((pairs * slots, LANES), f32),
            pltpu.VMEM((slots, pixels), bf16),
            pltpu.VMEM((slots, n_par), f32),
            pltpu.VMEM((n_epoch, per, n_par), f32),
            pltpu.VMEM((per, n_par), f32),
            pltpu.VMEM((n_sky * ratio, per, n_par), f32),
            dma((n_sky,)),
            dma((n_sky,)),
            dma((2, 2)),
            dma((2, 2)),
            dma((2,)),
            dma((2,)),
            dma((n_epoch,)),
            dma((n_epoch,)),
            dma((n_epoch,)),
            dma((n_sky * ratio,)),
        ],
        compiler_params=pltpu.CompilerParams(
            collective_id=0, has_side_effects=True, vmem_limit_bytes=48 * 1024 * 1024
        ),
    )(
        params,
        basis,
        psf_taps,
        psf_taps,
        send_index,
        tile_count,
        stamp_row,
        stamp_col,
        observed,
        background,
    )


def solution(mesh):
    in_specs = (
        P("sky", None),
        P(),
        P("epoch", None, None),
        P("sky", None, None),
        P("sky", None),
        P("sky", None, None),
        P("sky", None, None),
        P("epoch", "sky", None),
        P("epoch", "sky", None),
    )
    out_specs = (P("sky", None), P("epoch", "sky", None))
    return jax.shard_map(
        functools.partial(on_device, mesh.shape["sky"], mesh.shape["epoch"]),
        mesh=mesh,
        in_specs=in_specs,
        out_specs=out_specs,
        check_vma=False,
    )
```

time: 159 us -> 42.3 us (0.27)
  local copies, waits for them, and re-layouts: 60.4 us -> 5.48 us
  Pallas kernels: 0 us -> 35.8 us
  blocking collectives: 26 us -> 0 us
  matrix products: 23.4 us -> 0 us
  waiting for transfers between devices: 21.1 us -> 0 us
  starting transfers between devices: 19 us -> 0 us
  other arithmetic: 7.31 us -> 0 us
    gather x5 -> x0, local copies, waits for them, and re-layouts: 50.2 us -> none  [the longest x4 49.5 us: toeplitz(): taps[jnp.clip(where_at, 0, taps.shape[0] - 1)]]
    pallas_call x0 -> x1, Pallas kernels: none -> 35.8 us  [on_device(): pl.pallas_call(functools.partial(kernel, n_sky, n_epoch), out_shape=(jax....]
    psum x1 -> x0, blocking collectives: 26 us -> none  [on_device(): summed = lax.psum(slot_grad, 'epoch')]
    dot_general x15 -> x0, matrix products: 23.4 us -> none  [the longest x2 5.07 us: on_device(): jnp.einsum('ab,nbc,dc->nad', row_kernel, intrinsic, col_kernel, precision...]
    all_to_all x2 -> x0, waiting for transfers between devices: 12.7 us -> none  [the longest x1 6.46 us: on_device(): lax.all_to_all(patches.reshape(n_sky, capacity, -1), 'sky', split_axis=0,...]
    ppermute x4 -> x0, starting transfers between devices: 10.4 us -> none  [the longest x2 7.81 us: extended_2(): lax.ppermute(tail, axis, [(i, (i + 1) % count) for i in range(ends)])]
    all_to_all x2 -> x0, starting transfers between devices: 8.64 us -> none  [the longest x1 5.17 us: on_device(): lax.all_to_all(made, 'sky', split_axis=0, concat_axis=0, tiled=True)]
    ppermute x4 -> x0, waiting for transfers between devices: 8.43 us -> none  [the longest x2 8.22 us: extended_2(): lax.ppermute(head, axis, [((i + 1) % count, i) for i in range(ends)])]
  transfers between devices with their start and end apart: 6 -> 0, of which waited for: 5 -> 0; matrix products, arithmetic and copies ran while one was open for 2% -> 0% of each run, Pallas kernels for 0% -> 0%
where the time goes in v1:
time: 42.3 us; the launch traced here: 42 us
  Pallas kernels  35.8 us (85%)
  local copies, waits for them, and re-layouts  5.48 us (13%)
  between operations  0.73 us (2%)
    pallas_call x1, Pallas kernels, on_device(): pl.pallas_call(functools.partial(kernel, n_sky, n_epoch), out_shape=(jax....  35.8 us
    unnamed x18, local copies, waits for them, and re-layouts  4.79 us

profile of v1, /device:TPU:0, one launch (start us, length us, event | category | flops | bytes accessed | tf_op | source)
XLA Modules:
  0.0 42.0 jit_solution(15382604907974556675)
XLA Ops:
  0.6 0.0 copy-start.6
  0.6 0.0 copy-start.5
  0.7 0.0 copy-start.7
  0.7 0.0 copy-start.4
  0.7 0.0 copy-start.3
  0.7 0.9 %copy.11.params = bf16[128,64]{1,0:T(8,128)(2,1)S(1)} copy(bf16[128,64]{0,1:T(8,128)(2,1)} %param.9) | data formatting | bytes 32768 | tf_op args[0]
  1.5 0.0 copy-done.6
  1.5 0.0 copy-done.5
  1.6 0.0 copy-done.7
  1.6 0.0 copy-done.4
  1.6 0.0 copy-done.3
  1.6 0.0 copy-start
  1.6 1.0 %copy-done = bf16[64,4096]{1,0:T(8,128)(2,1)S(1)} copy-done((bf16[64,4096]{1,0:T(8,128)(2,1)S(1)}, bf16[64,4096]{1,0:T(8,128)(2,1)}, u32[]{:S(2)}) %copy-start) | copy-done | bytes 524312
  2.6 0.0 copy-start.1
  2.6 1.0 %copy-done.1 = f32[1,256,512]{2,1,0:T(8,128)S(1)} copy-done((f32[1,256,512]{2,1,0:T(8,128)S(1)}, f32[1,256,512]{2,1,0:T(8,128)}, u32[]{:S(2)}) %copy-start.1) | copy-done | bytes 524312
  3.7 0.0 copy-start.2
  3.7 1.0 %copy-done.2 = f32[1,256,512]{2,1,0:T(8,128)S(1)} copy-done((f32[1,256,512]{2,1,0:T(8,128)S(1)}, f32[1,256,512]{2,1,0:T(8,128)}, u32[]{:S(2)}) %copy-start.2) | copy-done | bytes 524312
  4.7 35.8 %shard_map.104 = (f32[128,64]{1,0:T(8,128)S(1)}, f32[1,256,512]{2,1,0:T(8,128)S(1)}) custom-call(bf16[128,64]{1,0:T(8,128)(2,1)S(1)} %copy.11.params, bf16[64,4096]{1,0:T(8,128)(2,1)S(1)} %copy-done, f32[1,2,51]{2,1,0:T(2,128)S(1)} %copy-done.3, f32[1,2,51]{2,1,0:T(2,128)S(1)} %copy-done.3, s32[1,4,16]{2,1,0:T(4,128)S(1)} %copy-done.4, ...), custom_call_target="tpu_custom_call" | custom-call | tf_op jit(solution)/shard_map/pallas_call | solution.py:535
  40.5 0.7 %copy.12 = f32[128,64]{0,1:T(8,128)} copy(f32[128,64]{1,0:T(8,128)S(1)} %get-tuple-element.2) | data formatting | bytes 65536 | tf_op jit(solution)/shard_map/pallas_call | solution.py:535
  41.2 0.8 %copy.14 = f32[1,256,512]{2,1,0:T(8,128)} copy(f32[1,256,512]{2,1,0:T(8,128)S(1)} %get-tuple-element.7) | data formatting | bytes 1048576
Async XLA Ops:
  0.6 0.9 %copy-start.6 = (s32[1,4,16]{2,1,0:T(4,128)S(1)}, s32[1,4,16]{2,1,0:T(4,128)}, u32[]{:S(2)}) copy-start(s32[1,4,16]{2,1,0:T(4,128)} %stamp_col.1) | copy-start | bytes 772
  0.6 0.9 %copy-start.5 = (s32[1,4,16]{2,1,0:T(4,128)S(1)}, s32[1,4,16]{2,1,0:T(4,128)}, u32[]{:S(2)}) copy-start(s32[1,4,16]{2,1,0:T(4,128)} %stamp_row.1) | copy-start | bytes 772
  0.7 0.9 %copy-start.7 = (s32[1,4]{1,0:T(1,128)S(1)}, s32[1,4]{1,0:T(1,128)}, u32[]{:S(2)}) copy-start(s32[1,4]{1,0:T(1,128)} %tile_count.1) | copy-start | bytes 52
  0.7 0.9 %copy-start.4 = (s32[1,4,16]{2,1,0:T(4,128)S(1)}, s32[1,4,16]{2,1,0:T(4,128)}, u32[]{:S(2)}) copy-start(s32[1,4,16]{2,1,0:T(4,128)} %send_index.1) | copy-start | bytes 772
  0.7 0.9 %copy-start.3 = (f32[1,2,51]{2,1,0:T(2,128)S(1)}, f32[1,2,51]{2,1,0:T(2,128)}, u32[]{:S(2)}) copy-start(f32[1,2,51]{2,1,0:T(2,128)} %taps_vector.1) | copy-start | bytes 1228
  1.6 1.0 %copy-start = (bf16[64,4096]{1,0:T(8,128)(2,1)S(1)}, bf16[64,4096]{1,0:T(8,128)(2,1)}, u32[]{:S(2)}) copy-start(bf16[64,4096]{1,0:T(8,128)(2,1)} %basis.1) | copy-start | bytes 1572868
  2.6 1.0 %copy-start.1 = (f32[1,256,512]{2,1,0:T(8,128)S(1)}, f32[1,256,512]{2,1,0:T(8,128)}, u32[]{:S(2)}) copy-start(f32[1,256,512]{2,1,0:T(8,128)} %observed.1) | copy-start | bytes 1572868
  3.7 1.0 %copy-start.2 = (f32[1,256,512]{2,1,0:T(8,128)S(1)}, f32[1,256,512]{2,1,0:T(8,128)}, u32[]{:S(2)}) copy-start(f32[1,256,512]{2,1,0:T(8,128)} %background.1) | copy-start | bytes 1572868

commit v2 on v1

--- a/solution.py
+++ b/solution.py
@@ -14,6 +14,10 @@
 def split_two(value):
     high = value.astype(jnp.bfloat16)
     return high, (value - high.astype(jnp.float32)).astype(jnp.bfloat16)
+
+
+def wrapped(value, count):
+    return jnp.where(value >= count, value - count, value)
 
 
 def wide_dot(left, right, dims=(((1,), (0,)), ((), ()))):
@@ -39,6 +43,9 @@
     incoming,
     observed_halo,
     background_halo,
+    basis_here,
+    observed_here,
+    background_here,
     basis_rows,
     basis_mixed,
     rendered_rows,
@@ -46,15 +53,16 @@
     stamps,
     row_one,
     moved,
-    canvas,
+    edges,
+    middle,
     light_halo,
     reach,
-    window_rows,
     windows,
     slot_grad,
     reduce_in,
     piece,
     gather_in,
+    load_sem,
     param_send,
     param_recv,
     halo_send,
@@ -68,7 +76,7 @@
 ):
     me_s = lax.axis_index("sky")
     me_e = lax.axis_index("epoch")
-    n_par = params.shape[1]
+    n_par, n_source = params.shape
     size = 64
     half = size // 2
     capacity = send_index.shape[2]
@@ -84,17 +92,33 @@
     n_taps = taps_vector.shape[2]
     reach_taps = (n_taps - 1) // 2
     my_owner = me_e // ratio
+    slot_pitch = slots + 8
+    par_pitch = n_par + 8
     has_above = me_s > 0
     has_below = me_s < n_sky - 1
+
+    loads = [
+        pltpu.make_async_copy(
+            basis.at[pl.ds(part * (n_par // 4), n_par // 4)],
+            basis_here.at[pl.ds(part * (n_par // 4), n_par // 4)],
+            load_sem.at[part],
+        )
+        for part in range(4)
+    ] + [
+        pltpu.make_async_copy(observed.at[0], observed_here, load_sem.at[4]),
+        pltpu.make_async_copy(background.at[0], background_here, load_sem.at[5]),
+    ]
+    for load in loads:
+        load.start()
 
     barrier = pltpu.get_barrier_semaphore()
     for step in range(1, n_sky):
         pl.semaphore_signal(
-            barrier, 1, device_id=(lax.rem(me_s + step, n_sky), me_e), device_id_type=MESH
+            barrier, 1, device_id=(wrapped(me_s + step, n_sky), me_e), device_id_type=MESH
         )
     for step in range(1, n_epoch):
         pl.semaphore_signal(
-            barrier, 1, device_id=(me_s, lax.rem(me_e + step, n_epoch)), device_id_type=MESH
+            barrier, 1, device_id=(me_s, wrapped(me_e + step, n_epoch)), device_id_type=MESH
         )
     for tile in range(n_sky):
         for part in range(ratio):
@@ -104,24 +128,25 @@
             def _():
                 pl.semaphore_signal(barrier, 1, device_id=(tile, sender), device_id_type=MESH)
 
-    slot_at = lax.broadcasted_iota(jnp.int32, (slots, params.shape[0]), 0)
-    source_at = lax.broadcasted_iota(jnp.int32, (slots, params.shape[0]), 1)
-    named = jnp.zeros_like(slot_at)
-    for tile in range(n_sky):
-        for k in range(capacity):
-            named = jnp.where(slot_at == tile * capacity + k, send_index[0, tile, k], named)
-    picked = wide_dot((named == source_at).astype(jnp.bfloat16), params[...]).astype(jnp.bfloat16)
+    slot_at = lax.broadcasted_iota(jnp.int32, (8, n_source), 0)
+    source_at = lax.broadcasted_iota(jnp.int32, (8, n_source), 1)
+    rows_of = []
+    for base in range(0, slots, 8):
+        named = jnp.zeros_like(slot_at)
+        for inner in range(8):
+            tile, k = divmod(base + inner, capacity)
+            named = jnp.where(slot_at == inner, send_index[0, tile, k], named)
+        rows_of.append(jnp.where(named == source_at, 1.0, 0.0))
+    table = jnp.concatenate(rows_of, axis=0)
+    picked = wide_dot(
+        table.astype(jnp.bfloat16), params[...], (((1,), (1,)), ((), ()))
+    ).astype(jnp.bfloat16)
     for tile in range(n_sky):
         outgoing[tile] = picked[tile * capacity : (tile + 1) * capacity]
     incoming[me_s] = outgoing[me_s]
 
-    pl.semaphore_wait(
-        barrier,
-        (n_sky - 1) + (n_epoch - 1) + n_epoch - jnp.where(my_owner == me_s, 1, 0),
-    )
-
     def param_copy(step):
-        other = lax.rem(me_s + step, n_sky)
+        other = wrapped(me_s + step, n_sky)
         return pltpu.make_async_remote_copy(
             src_ref=outgoing.at[other],
             dst_ref=incoming.at[me_s],
@@ -151,10 +176,10 @@
 
     def light_copy(upward):
         other = me_s - 1 if upward else me_s + 1
-        start = 0 if upward else canvas_rows - 2 * margin
+        start = 0 if upward else 2 * margin
         slot = 1 if upward else 0
         return pltpu.make_async_remote_copy(
-            src_ref=canvas.at[pl.ds(start, 2 * margin)],
+            src_ref=edges.at[pl.ds(start, 2 * margin)],
             dst_ref=light_halo.at[slot],
             send_sem=light_send.at[slot],
             recv_sem=light_recv.at[slot],
@@ -162,19 +187,6 @@
             device_id_type=MESH,
         )
 
-    for step in range(1, n_sky):
-        param_copy(step).start()
-
-    @pl.when(has_above)
-    def _():
-        for copy in halo_copies(True):
-            copy.start()
-
-    @pl.when(has_below)
-    def _():
-        for copy in halo_copies(False):
-            copy.start()
-
     @pl.when(jnp.logical_not(has_above))
     def _():
         light_halo[0] = jnp.zeros(light_halo.shape[1:], jnp.float32)
@@ -188,7 +200,7 @@
         background_halo[1] = jnp.ones(background_halo.shape[1:], jnp.float32)
 
     def natural(value):
-        return 2 * (value % half) + value // half
+        return 2 * (value & (half - 1)) + (value >> 5)
 
     row_a = natural(lax.broadcasted_iota(jnp.int32, (size, size), 0))
     row_b = natural(lax.broadcasted_iota(jnp.int32, (size, size), 1))
@@ -196,7 +208,9 @@
     col_c = lax.broadcasted_iota(jnp.int32, (LANES, LANES), 0)
     col_d = lax.broadcasted_iota(jnp.int32, (LANES, LANES), 1)
     col_where = jnp.where(
-        col_c // size == col_d // size, col_d % size - col_c % size + reach_taps, -1
+        (col_c >> 6) == (col_d >> 6),
+        (col_d & (size - 1)) - (col_c & (size - 1)) + reach_taps,
+        -1,
     )
 
     def tap_step(tap, both):
@@ -216,10 +230,38 @@
     total = jnp.sum(taps_vector[0], axis=1, keepdims=True)
     row_high, row_low = split_two(row_k / total[0:1])
     col_high, col_low = split_two(col_k / total[1:2])
-
+    row_both = jnp.concatenate([row_high, row_low], axis=0)
+    col_both = jnp.concatenate(
+        [
+            jnp.concatenate([col_high, col_low], axis=1),
+            jnp.concatenate([col_high, jnp.zeros_like(col_low)], axis=1),
+        ],
+        axis=0,
+    )
+
+    pl.semaphore_wait(
+        barrier,
+        (n_sky - 1) + (n_epoch - 1) + n_epoch - jnp.where(my_owner == me_s, 1, 0),
+    )
+
+    for step in range(1, n_sky):
+        param_copy(step).start()
+
+    @pl.when(has_above)
+    def _():
+        for copy in halo_copies(True):
+            copy.start()
+
+    @pl.when(has_below)
+    def _():
+        for copy in halo_copies(False):
+            copy.start()
+
+    for load in loads[:4]:
+        load.wait()
     lane_half = lax.broadcasted_iota(jnp.int32, (half, LANES), 1) < size
     for pair in range(pairs):
-        basis_rows[pl.ds(pair * n_par, n_par), :] = basis[
+        basis_rows[pl.ds(pair * par_pitch, n_par), :] = basis_here[
             :, pair * LANES : (pair + 1) * LANES
         ].astype(jnp.float32)
 
@@ -234,30 +276,32 @@
     def mix_group(index, carry):
         for inner in range(group):
             pp = index * group + inner
-            one = basis_rows[pl.ds(2 * pp, half, stride=n_par), :]
-            two = basis_rows[pl.ds(2 * pp + 1, half, stride=n_par), :]
+            one = basis_rows[pl.ds(2 * pp, half, stride=par_pitch), :]
+            two = basis_rows[pl.ds(2 * pp + 1, half, stride=par_pitch), :]
             first, second = swapped(one, two)
             lanes = pl.ds(inner * LANES, LANES)
             basis_mixed[:half, lanes] = first.astype(jnp.bfloat16)
             basis_mixed[half:, lanes] = second.astype(jnp.bfloat16)
         mixed = basis_mixed[...]
-        by_row = wide_dot(row_high, mixed) + wide_dot(row_low, mixed)
+        by_row = wide_dot(row_both, mixed)
+        by_row = by_row[:size] + by_row[size:]
         tall = jnp.concatenate(
             [by_row[:, inner * LANES : (inner + 1) * LANES] for inner in range(group)], axis=0
         )
         high, low = split_two(tall)
-        done = wide_dot(high, col_high) + (wide_dot(low, col_high) + wide_dot(high, col_low))
+        done = wide_dot(jnp.concatenate([high, low], axis=1), col_both)
+        done = done[:, :LANES] + done[:, LANES:]
         for inner in range(group):
             pp = index * group + inner
             base = inner * size
             first, second = swapped(done[base : base + half], done[base + half : base + size])
-            rendered_rows[pl.ds(2 * pp, half, stride=n_par), :] = first
-            rendered_rows[pl.ds(2 * pp + 1, half, stride=n_par), :] = second
+            rendered_rows[pl.ds(2 * pp, half, stride=par_pitch), :] = first
+            rendered_rows[pl.ds(2 * pp + 1, half, stride=par_pitch), :] = second
         return carry
 
     lax.fori_loop(0, n_par // 2 // group, mix_group, 0)
     for pair in range(pairs):
-        high, low = split_two(rendered_rows[pl.ds(pair * n_par, n_par), :])
+        high, low = split_two(rendered_rows[pl.ds(pair * par_pitch, n_par), :])
         rendered[:n_par, pair * LANES : (pair + 1) * LANES] = high
         rendered[n_par:, pair * LANES : (pair + 1) * LANES] = low
 
@@ -272,50 +316,64 @@
         )
         live = jnp.where(inside & (par_slot < (owner + 1) * capacity), 1.0, live)
     here = incoming[...].reshape(slots, n_par).astype(jnp.float32)
-    here = jnp.where(live > 0, here, 0.0).astype(jnp.bfloat16)
+    here = jnp.where(live > 0, here, 0.0)
+    here = jnp.concatenate([here, here], axis=1).astype(jnp.bfloat16)
     wide = 8
     for block in range(pairs // wide):
         lanes = slice(block * wide * LANES, (block + 1) * wide * LANES)
-        made = wide_dot(here, rendered[:n_par, lanes]) + wide_dot(here, rendered[n_par:, lanes])
+        made = wide_dot(here, rendered[:, lanes])
         for inner in range(wide):
-            stamps[pl.ds((block * wide + inner) * slots, slots), :] = made[
+            stamps[pl.ds((block * wide + inner) * slot_pitch, slots), :] = made[
                 :, inner * LANES : (inner + 1) * LANES
             ]
 
     lane_row = lax.broadcasted_iota(jnp.int32, (1, LANES), 1)
     level = lax.broadcasted_iota(jnp.int32, (canvas_rows, LANES), 0)
-    offset = level - natural(lax.broadcasted_iota(jnp.int32, (canvas_rows, LANES), 1) % size)
-    canvas[...] = jnp.zeros_like(canvas)
+    level = jnp.where(
+        level < 2 * margin,
+        level,
+        jnp.where(level < 4 * margin, level + (canvas_rows - 4 * margin), level - 2 * margin),
+    )
+    offset = level - natural(lane_row & (size - 1))
+    span = capacity * size
 
     def place_owner(owner, carry):
-        def place_pair(pair, inner_carry):
+        base = pl.multiple_of(owner * span, span)
+        for pair in range(capacity // 2):
             rows = []
             for which in range(2):
                 k = 2 * pair + which
                 col = stamp_col[0, owner, k]
                 rows.append(stamp_row[0, owner, k])
-                stamp = stamps[pl.ds(owner * capacity + k, half, stride=slots), :]
-                shift = lax.rem(col, LANES)
-                even = pltpu.roll(stamp, shift, 1)
+                stamp = stamps[pl.ds(owner * capacity + k, half, stride=slot_pitch), :]
+                even = pltpu.roll(stamp, col & (LANES - 1), 1)
                 odd = pltpu.roll(even, size, 1)
                 for plane in range(planes):
                     at = lane_row + (plane * LANES) - col
                     inside = (at >= 0) & (at < size)
                     for parity, data in enumerate((even, odd)):
-                        start = pl.multiple_of(k * size + parity * half, half)
-                        moved[pl.ds(start, half), plane * LANES : (plane + 1) * LANES] = jnp.where(
-                            inside, data, 0.0
-                        ).astype(jnp.bfloat16)
+                        moved[
+                            pl.ds(base + k * size + parity * half, half),
+                            plane * LANES : (plane + 1) * LANES,
+                        ] = jnp.where(inside, data, 0.0).astype(jnp.bfloat16)
             target = jnp.where(lane_row < size, rows[0], rows[1])
-            lanes = pl.ds(pl.multiple_of(pair * LANES, LANES), LANES)
-            row_one[:, lanes] = jnp.where(offset == target, 1.0, 0.0).astype(jnp.bfloat16)
-            return inner_carry
-
-        lax.fori_loop(0, capacity // 2, place_pair, 0, unroll=2)
-        canvas[...] += wide_dot(row_one[...], moved[...])
+            row_one[:, pl.ds(base + pair * LANES, LANES)] = jnp.where(
+                offset == target, 1.0, 0.0
+            ).astype(jnp.bfloat16)
         return carry
 
     lax.fori_loop(0, n_sky, place_owner, 0)
+    run = 2 * span if n_sky % 2 == 0 else span
+
+    def gathered(rows):
+        def add(index, sum_so_far):
+            depth = pl.ds(pl.multiple_of(index * run, run), run)
+            return sum_so_far + wide_dot(row_one[rows, depth], moved[depth, :])
+
+        first = wide_dot(row_one[rows, :run], moved[:run, :])
+        return lax.fori_loop(1, n_sky * span // run, add, first)
+
+    edges[...] = gathered(slice(0, 4 * margin))
 
     @pl.when(has_above)
     def _():
@@ -338,20 +396,23 @@
                 :, plane * LANES : (plane + 1) * LANES
             ]
 
+    middle[...] = gathered(slice(4 * margin, canvas_rows))
+    for load in loads[4:]:
+        load.wait()
+
     def core_chunk(index, carry):
         start = pl.multiple_of(index * margin, margin)
-        inner = pl.multiple_of(start - margin, margin)
+        inner = pl.multiple_of(start + margin, margin)
         value = residual_of(
-            canvas[pl.ds(start, margin), :],
-            observed[0, pl.ds(inner, margin), :],
-            background[0, pl.ds(inner, margin), :],
+            middle[pl.ds(start, margin), :],
+            observed_here[pl.ds(inner, margin), :],
+            background_here[pl.ds(inner, margin), :],
         )
         residual_out[0, pl.ds(inner, margin), :] = value
-        keep(value, start)
+        keep(value, pl.multiple_of(start + 2 * margin, margin))
         return carry
 
-    chunks = canvas_rows // margin
-    lax.fori_loop(2, chunks - 2, core_chunk, 0)
+    lax.fori_loop(0, canvas_rows // margin - 4, core_chunk, 0)
     reach[planes * canvas_rows :, :] = jnp.zeros((canvas_rows, LANES), jnp.float32)
 
     @pl.when(has_above)
@@ -378,15 +439,17 @@
         outer_light = 0 if slot == 0 else margin
         inner_light = margin - outer_light
         value = residual_of(
-            canvas[pl.ds(outer, margin), :] + light_halo[slot, pl.ds(outer_light, margin), :],
+            edges[pl.ds(2 * slot * margin + outer_light, margin), :]
+            + light_halo[slot, pl.ds(outer_light, margin), :],
             observed_halo[slot],
             background_halo[slot],
         )
         keep(jnp.where(exists, value, 0.0), outer)
         value = residual_of(
-            canvas[pl.ds(inner, margin), :] + light_halo[slot, pl.ds(inner_light, margin), :],
-            observed[0, pl.ds(inner - margin, margin), :],
-            background[0, pl.ds(inner - margin, margin), :],
+            edges[pl.ds(2 * slot * margin + inner_light, margin), :]
+            + light_halo[slot, pl.ds(inner_light, margin), :],
+            observed_here[pl.ds(inner - margin, margin), :],
+            background_here[pl.ds(inner - margin, margin), :],
         )
         residual_out[0, pl.ds(inner - margin, margin), :] = value
         keep(value, inner)
@@ -395,9 +458,9 @@
         def pick(k, inner_carry):
             col = stamp_col[0, owner, k]
             row = stamp_row[0, owner, k]
-            shift = lax.rem(col, LANES)
-            first = (col // LANES) * canvas_rows + row
-            back = lax.rem(LANES - shift, LANES)
+            shift = col & (LANES - 1)
+            first = (col >> 7) * canvas_rows + row
+            back = (LANES - shift) & (LANES - 1)
             halves = []
             for parity in range(2):
                 near = reach[pl.ds(first + parity, half, stride=2), :]
@@ -405,23 +468,23 @@
                 halves.append(jnp.where(lane_row >= shift, near, far))
             even = pltpu.roll(halves[0], back, 1)
             odd = pltpu.roll(pltpu.roll(halves[1], back, 1), size, 1)
-            window_rows[pl.ds(owner * capacity + k, half, stride=slots), :] = jnp.where(
+            stamps[pl.ds(owner * capacity + k, half, stride=slot_pitch), :] = jnp.where(
                 lane_half, even, odd
             )
             return inner_carry
 
-        return lax.fori_loop(0, capacity, pick, carry, unroll=4)
+        return lax.fori_loop(0, capacity, pick, carry, unroll=capacity)
 
     lax.fori_loop(0, n_sky, pick_owner, 0)
     for pair in range(pairs):
-        windows[:, pair * LANES : (pair + 1) * LANES] = window_rows[
-            pl.ds(pair * slots, slots), :
+        windows[:, pair * LANES : (pair + 1) * LANES] = stamps[
+            pl.ds(pair * slot_pitch, slots), :
         ].astype(jnp.bfloat16)
     both = wide_dot(windows[...], rendered[...], (((1,), (1,)), ((), ())))
     slot_grad[...] = jnp.where(live > 0, both[:, :n_par] + both[:, n_par:], 0.0)
 
     def reduce_copy(step):
-        other = lax.rem(me_e + step, n_epoch)
+        other = wrapped(me_e + step, n_epoch)
         return pltpu.make_async_remote_copy(
             src_ref=slot_grad.at[pl.ds(pl.multiple_of(other * per, per), per)],
             dst_ref=reduce_in.at[step],
@@ -446,7 +509,7 @@
             dst_ref=gather_in.at[my_place],
             send_sem=gather_send.at[step],
             recv_sem=gather_recv.at[my_place],
-            device_id=(my_owner, lax.rem(me_e + step, n_epoch)),
+            device_id=(my_owner, wrapped(me_e + step, n_epoch)),
             device_id_type=MESH,
         )
 
@@ -460,16 +523,6 @@
     @pl.when(my_owner != me_s)
     def _():
         gather_copy(0).start()
-
-    out_source = lax.broadcasted_iota(jnp.int32, (params.shape[0], slots), 0)
-    out_slot = lax.broadcasted_iota(jnp.int32, (1, slots), 1)
-    out_named = jnp.zeros((1, slots), jnp.int32)
-    for tile in range(n_sky):
-        for k in range(capacity):
-            out_named = jnp.where(
-                out_slot == tile * capacity + k, send_index[0, tile, k], out_named
-            )
-    table = (out_source == out_named).astype(jnp.float32)
 
     for step in range(1, n_epoch):
         reduce_copy(step).wait_send()
@@ -496,9 +549,9 @@
 
     back = gather_in[...].reshape(slots, n_par)
     grad_out[...] = lax.dot_general(
+        back,
         table,
-        back,
-        (((1,), (0,)), ((), ())),
+        (((0,), (0,)), ((), ())),
         precision=lax.Precision.HIGHEST,
         preferred_element_type=jnp.float32,
     )
@@ -532,35 +585,40 @@
     vmem = pl.BlockSpec(memory_space=pltpu.VMEM)
     smem = pl.BlockSpec(memory_space=pltpu.SMEM)
     dma = pltpu.SemaphoreType.DMA
-    return pl.pallas_call(
+    hbm = pl.BlockSpec(memory_space=pltpu.HBM)
+    param_grad, residual = pl.pallas_call(
         functools.partial(kernel, n_sky, n_epoch),
         out_shape=(
-            jax.ShapeDtypeStruct((params.shape[0], n_par), f32),
+            jax.ShapeDtypeStruct((n_par, params.shape[0]), f32),
             jax.ShapeDtypeStruct(observed.shape, f32),
         ),
-        in_specs=[vmem, vmem, smem, vmem, smem, smem, smem, smem, vmem, vmem],
+        in_specs=[vmem, hbm, smem, vmem, smem, smem, smem, smem, hbm, hbm],
         out_specs=(vmem, vmem),
         scratch_shapes=[
             pltpu.VMEM((n_sky, capacity, n_par), bf16),
             pltpu.VMEM((n_sky, capacity, n_par), bf16),
             pltpu.VMEM((2, margin, width), f32),
             pltpu.VMEM((2, margin, width), f32),
-            pltpu.VMEM((pairs * n_par, LANES), f32),
+            pltpu.VMEM((n_par, pixels), bf16),
+            pltpu.VMEM((tile_rows, width), f32),
+            pltpu.VMEM((tile_rows, width), f32),
+            pltpu.VMEM((pairs * (n_par + 8), LANES), f32),
             pltpu.VMEM((size, 8 * LANES), bf16),
-            pltpu.VMEM((pairs * n_par, LANES), f32),
+            pltpu.VMEM((pairs * (n_par + 8), LANES), f32),
             pltpu.VMEM((2 * n_par, pixels), bf16),
-            pltpu.VMEM((pairs * slots, LANES), f32),
-            pltpu.VMEM((canvas_rows, capacity * size), bf16),
-            pltpu.VMEM((capacity * size, width), bf16),
-            pltpu.VMEM((canvas_rows, width), f32),
+            pltpu.VMEM((pairs * (slots + 8), LANES), f32),
+            pltpu.VMEM((canvas_rows, slots * size), bf16),
+            pltpu.VMEM((slots * size, width), bf16),
+            pltpu.VMEM((4 * margin, width), f32),
+            pltpu.VMEM((tile_rows - 2 * margin, width), f32),
             pltpu.VMEM((2, 2 * margin, width), f32),
             pltpu.VMEM(((planes + 1) * canvas_rows, LANES), f32),
-            pltpu.VMEM((pairs * slots, LANES), f32),
             pltpu.VMEM((slots, pixels), bf16),
             pltpu.VMEM((slots, n_par), f32),
             pltpu.VMEM((n_epoch, per, n_par), f32),
             pltpu.VMEM((per, n_par), f32),
             pltpu.VMEM((n_sky * ratio, per, n_par), f32),
+            dma((6,)),
             dma((n_sky,)),
             dma((n_sky,)),
             dma((2, 2)),
@@ -573,10 +631,10 @@
             dma((n_sky * ratio,)),
         ],
         compiler_params=pltpu.CompilerParams(
-            collective_id=0, has_side_effects=True, vmem_limit_bytes=48 * 1024 * 1024
+            collective_id=0, has_side_effects=True, vmem_limit_bytes=56 * 1024 * 1024
         ),
     )(
-        params,
+        params.T,
         basis,
         psf_taps,
         psf_taps,
@@ -587,6 +645,7 @@
         observed,
         background,
     )
+    return param_grad.T, residual
 
 
 def solution(mesh):

time: 42.3 us -> 35.5 us (0.84)
  Pallas kernels: 35.8 us -> 31.3 us
  local copies, waits for them, and re-layouts: 5.48 us -> 3.24 us
    pallas_call x1, Pallas kernels: 35.8 us -> 31.3 us  [on_device(): pl.pallas_call(functools.partial(kernel, n_sky, n_epoch), out_shape=(jax....]
    unnamed x18 -> x2, local copies, waits for them, and re-layouts: 4.79 us -> 3.24 us
    pallas_call x1 -> x0, local copies, waits for them, and re-layouts: 0.7 us -> none  [on_device(): pl.pallas_call(functools.partial(kernel, n_sky, n_epoch), out_shape=(jax....]
where the time goes in v2:
time: 35.5 us; the launch traced here: 35.2 us
  Pallas kernels  31.3 us (88%)
  local copies, waits for them, and re-layouts  3.24 us (9%)
  between operations  0.64 us (2%)
    pallas_call x1, Pallas kernels, on_device(): pl.pallas_call(functools.partial(kernel, n_sky, n_epoch), out_shape=(jax....  31.3 us
    unnamed x2, local copies, waits for them, and re-layouts  3.24 us

profile of v2, /device:TPU:0, one launch (start us, length us, event | category | flops | bytes accessed | tf_op | source)
XLA Modules:
  0.0 35.2 jit_solution(15127359465225316308)
XLA Ops:
  0.6 31.3 %shard_map.104 = (f32[64,128]{1,0:T(8,128)}, f32[1,256,512]{2,1,0:T(8,128)}) custom-call(bf16[64,128]{1,0:T(8,128)(2,1)} %bitcast.3, bf16[64,4096]{1,0:T(8,128)(2,1)} %basis.1, f32[1,2,51]{2,1,0:T(2,128)} %taps_vector.1, f32[1,2,51]{2,1,0:T(2,128)} %taps_vector.1, s32[1,4,16]{2,1,0:T(4,128)} %send_index.1, s32[1,4]{1,0:T(1,128)} %tile_count.1, ...), custom_call_target="tpu_custom_call" | custom-call | tf_op jit(solution)/shard_map/pallas_call | solution.py:589
  32.0 1.4 %copy.13 = f32[128,64]{0,1:T(8,128)} copy(f32[128,64]{0,1:T(8,128)} %bitcast.2) | data formatting | bytes 65536
  33.3 1.9 %copy.14 = f32[1,256,512]{2,1,0:T(8,128)} copy(f32[1,256,512]{2,1,0:T(8,128)} %get-tuple-element.9) | data formatting | bytes 1048576

commit v3 on v2

--- a/solution.py
+++ b/solution.py
@@ -205,13 +205,9 @@
     row_a = natural(lax.broadcasted_iota(jnp.int32, (size, size), 0))
     row_b = natural(lax.broadcasted_iota(jnp.int32, (size, size), 1))
     row_where = row_a - row_b + reach_taps
-    col_c = lax.broadcasted_iota(jnp.int32, (LANES, LANES), 0)
-    col_d = lax.broadcasted_iota(jnp.int32, (LANES, LANES), 1)
-    col_where = jnp.where(
-        (col_c >> 6) == (col_d >> 6),
-        (col_d & (size - 1)) - (col_c & (size - 1)) + reach_taps,
-        -1,
-    )
+    col_c = lax.broadcasted_iota(jnp.int32, (size, size), 0)
+    col_d = lax.broadcasted_iota(jnp.int32, (size, size), 1)
+    col_where = col_d - col_c + reach_taps
 
     def tap_step(tap, both):
         row_k, col_k = both
@@ -224,12 +220,17 @@
         0,
         n_taps,
         tap_step,
-        (jnp.zeros((size, size), jnp.float32), jnp.zeros((LANES, LANES), jnp.float32)),
-        unroll=3,
+        (jnp.zeros((size, size), jnp.float32), jnp.zeros((size, size), jnp.float32)),
+        unroll=17 if n_taps % 17 == 0 else 1,
     )
     total = jnp.sum(taps_vector[0], axis=1, keepdims=True)
     row_high, row_low = split_two(row_k / total[0:1])
-    col_high, col_low = split_two(col_k / total[1:2])
+    col_k = col_k / total[1:2]
+    blank = jnp.zeros_like(col_k)
+    col_k = jnp.concatenate(
+        [jnp.concatenate([col_k, blank], axis=1), jnp.concatenate([blank, col_k], axis=1)], axis=0
+    )
+    col_high, col_low = split_two(col_k)
     row_both = jnp.concatenate([row_high, row_low], axis=0)
     col_both = jnp.concatenate(
         [
@@ -273,17 +274,18 @@
 
     group = 8
 
-    def mix_group(index, carry):
+    for index in range(n_par // 2 // group):
         for inner in range(group):
             pp = index * group + inner
             one = basis_rows[pl.ds(2 * pp, half, stride=par_pitch), :]
             two = basis_rows[pl.ds(2 * pp + 1, half, stride=par_pitch), :]
             first, second = swapped(one, two)
-            lanes = pl.ds(inner * LANES, LANES)
-            basis_mixed[:half, lanes] = first.astype(jnp.bfloat16)
-            basis_mixed[half:, lanes] = second.astype(jnp.bfloat16)
-        mixed = basis_mixed[...]
-        by_row = wide_dot(row_both, mixed)
+            basis_mixed[:half, pp * LANES : (pp + 1) * LANES] = first.astype(jnp.bfloat16)
+            basis_mixed[half:, pp * LANES : (pp + 1) * LANES] = second.astype(jnp.bfloat16)
+    for index in range(n_par // 2 // group):
+        by_row = wide_dot(
+            row_both, basis_mixed[:, index * group * LANES : (index + 1) * group * LANES]
+        )
         by_row = by_row[:size] + by_row[size:]
         tall = jnp.concatenate(
             [by_row[:, inner * LANES : (inner + 1) * LANES] for inner in range(group)], axis=0
@@ -297,9 +299,6 @@
             first, second = swapped(done[base : base + half], done[base + half : base + size])
             rendered_rows[pl.ds(2 * pp, half, stride=par_pitch), :] = first
             rendered_rows[pl.ds(2 * pp + 1, half, stride=par_pitch), :] = second
-        return carry
-
-    lax.fori_loop(0, n_par // 2 // group, mix_group, 0)
     for pair in range(pairs):
         high, low = split_two(rendered_rows[pl.ds(pair * par_pitch, n_par), :])
         rendered[:n_par, pair * LANES : (pair + 1) * LANES] = high
@@ -412,7 +411,7 @@
         keep(value, pl.multiple_of(start + 2 * margin, margin))
         return carry
 
-    lax.fori_loop(0, canvas_rows // margin - 4, core_chunk, 0)
+    lax.fori_loop(0, canvas_rows // margin - 4, core_chunk, 0, unroll=3)
     reach[planes * canvas_rows :, :] = jnp.zeros((canvas_rows, LANES), jnp.float32)
 
     @pl.when(has_above)
@@ -548,13 +547,32 @@
                 ).wait_recv()
 
     back = gather_in[...].reshape(slots, n_par)
-    grad_out[...] = lax.dot_general(
-        back,
-        table,
+    high = back.astype(jnp.bfloat16)
+    rest = back - high.astype(jnp.float32)
+    middle_part, low = split_two(rest)
+    exact = table.astype(jnp.bfloat16)
+    grad_out[...] = wide_dot(
+        jnp.concatenate([high, middle_part, low], axis=0),
+        jnp.concatenate([exact, exact, exact], axis=0),
         (((0,), (0,)), ((), ())),
-        precision=lax.Precision.HIGHEST,
-        preferred_element_type=jnp.float32,
-    )
+    )
+
+
+def finish(grad, residual, grad_out, residual_out, sems):
+    parts = 4
+    rows = residual.shape[1] // parts
+    copies = [
+        pltpu.make_async_copy(
+            residual.at[0, pl.ds(part * rows, rows)],
+            residual_out.at[0, pl.ds(part * rows, rows)],
+            sems.at[part],
+        )
+        for part in range(parts)
+    ] + [pltpu.make_async_copy(grad, grad_out, sems.at[parts])]
+    for copy in copies:
+        copy.start()
+    for copy in copies:
+        copy.wait()
 
 
 def on_device(
@@ -586,10 +604,18 @@
     smem = pl.BlockSpec(memory_space=pltpu.SMEM)
     dma = pltpu.SemaphoreType.DMA
     hbm = pl.BlockSpec(memory_space=pltpu.HBM)
+    params = params.T
+    params, basis, psf_taps, send_index, tile_count, stamp_row, stamp_col = (
+        pltpu.with_memory_space_constraint(array, pltpu.HBM)
+        for array in (params, basis, psf_taps, send_index, tile_count, stamp_row, stamp_col)
+    )
+    observed, background = (
+        pltpu.with_memory_space_constraint(array, pltpu.HBM) for array in (observed, background)
+    )
     param_grad, residual = pl.pallas_call(
         functools.partial(kernel, n_sky, n_epoch),
         out_shape=(
-            jax.ShapeDtypeStruct((n_par, params.shape[0]), f32),
+            jax.ShapeDtypeStruct((n_par, params.shape[1]), f32),
             jax.ShapeDtypeStruct(observed.shape, f32),
         ),
         in_specs=[vmem, hbm, smem, vmem, smem, smem, smem, smem, hbm, hbm],
@@ -603,7 +629,7 @@
             pltpu.VMEM((tile_rows, width), f32),
             pltpu.VMEM((tile_rows, width), f32),
             pltpu.VMEM((pairs * (n_par + 8), LANES), f32),
-            pltpu.VMEM((size, 8 * LANES), bf16),
+            pltpu.VMEM((size, pixels), bf16),
             pltpu.VMEM((pairs * (n_par + 8), LANES), f32),
             pltpu.VMEM((2 * n_par, pixels), bf16),
             pltpu.VMEM((pairs * (slots + 8), LANES), f32),
@@ -631,10 +657,10 @@
             dma((n_sky * ratio,)),
         ],
         compiler_params=pltpu.CompilerParams(
-            collective_id=0, has_side_effects=True, vmem_limit_bytes=56 * 1024 * 1024
+            collective_id=0, has_side_effects=True, vmem_limit_bytes=(14 * 1024 + slots * 160) * 1024
         ),
     )(
-        params.T,
+        params,
         basis,
         psf_taps,
         psf_taps,
@@ -645,6 +671,16 @@
         observed,
         background,
     )
+    param_grad, residual = pl.pallas_call(
+        finish,
+        out_shape=(
+            jax.ShapeDtypeStruct(param_grad.shape, f32),
+            jax.ShapeDtypeStruct(residual.shape, f32),
+        ),
+        in_specs=[vmem, vmem],
+        out_specs=(hbm, hbm),
+        scratch_shapes=[dma((5,))],
+    )(param_grad, residual)
     return param_grad.T, residual
 
 

time: 35.5 us -> 34.8 us (0.980)
  local copies, waits for them, and re-layouts: 3.24 us -> 1.38 us
  Pallas kernels: 31.3 us -> 32.5 us
    pallas_call x0 -> x1, Pallas kernels: none -> 1.89 us  [on_device(): pl.pallas_call(finish, out_shape=(jax.ShapeDtypeStruct(param_grad.shape,...]
    unnamed x2 -> x4, local copies, waits for them, and re-layouts: 3.24 us -> 1.38 us
    pallas_call x1, Pallas kernels: 31.3 us -> 30.7 us  [on_device(): pl.pallas_call(functools.partial(kernel, n_sky, n_epoch), out_shape=(jax....]
where the time goes in v3:
time: 34.8 us; the launch traced here: 34.6 us
  Pallas kernels  32.5 us (93%)
  local copies, waits for them, and re-layouts  1.38 us (4%)
  between operations  0.65 us (2%)
    pallas_call x1, Pallas kernels, on_device(): pl.pallas_call(functools.partial(kernel, n_sky, n_epoch), out_shape=(jax....  30.7 us
    pallas_call x1, Pallas kernels, on_device(): pl.pallas_call(finish, out_shape=(jax.ShapeDtypeStruct(param_grad.shape,...  1.89 us
    unnamed x4, local copies, waits for them, and re-layouts  1.38 us

profile of v3, /device:TPU:0, one launch (start us, length us, event | category | flops | bytes accessed | tf_op | source)
XLA Modules:
  0.0 34.6 jit_solution(17576675600343653200)
XLA Ops:
  0.6 30.7 %shard_map.104 = (f32[64,128]{1,0:T(8,128)S(1)}, f32[1,256,512]{2,1,0:T(8,128)S(1)}) custom-call(bf16[64,128]{1,0:T(8,128)(2,1)} %bitcast.2, bf16[64,4096]{1,0:T(8,128)(2,1)} %basis.1, f32[1,2,51]{2,1,0:T(2,128)} %taps_vector.1, f32[1,2,51]{2,1,0:T(2,128)} %taps_vector.1, s32[1,4,16]{2,1,0:T(4,128)} %send_index.1, s32[1,4]{1,0:T(1,128)} %tile_count.1, ...), custom_call_target="tpu_custom_call" | custom-call | tf_op jit(solution)/shard_map/pallas_call | solution.py:615
  31.3 0.0 copy-start
  31.3 0.8 %copy-done = f32[1,256,512]{2,1,0:T(8,128)} copy-done((f32[1,256,512]{2,1,0:T(8,128)}, f32[1,256,512]{2,1,0:T(8,128)S(1)}, u32[]{:S(2)}) %copy-start) | copy-done | bytes 524312
  32.1 0.0 copy-start.1
  32.1 0.6 %copy-done.1 = f32[64,128]{1,0:T(8,128)} copy-done((f32[64,128]{1,0:T(8,128)}, f32[64,128]{1,0:T(8,128)S(1)}, u32[]{:S(2)}) %copy-start.1) | copy-done | bytes 32792
  32.7 1.9 %shard_map.105 = (f32[64,128]{1,0:T(8,128)}, f32[1,256,512]{2,1,0:T(8,128)}) custom-call(f32[64,128]{1,0:T(8,128)} %copy-done.1, f32[1,256,512]{2,1,0:T(8,128)} %copy-done), custom_call_target="tpu_custom_call" | custom-call | tf_op jit(solution)/shard_map/pallas_call | solution.py:674
Async XLA Ops:
  31.3 0.8 %copy-start = (f32[1,256,512]{2,1,0:T(8,128)}, f32[1,256,512]{2,1,0:T(8,128)S(1)}, u32[]{:S(2)}) copy-start(f32[1,256,512]{2,1,0:T(8,128)S(1)} %get-tuple-element.7.residual) | copy-start | bytes 1572868
  32.1 0.6 %copy-start.1 = (f32[64,128]{1,0:T(8,128)}, f32[64,128]{1,0:T(8,128)S(1)}, u32[]{:S(2)}) copy-start(f32[64,128]{1,0:T(8,128)S(1)} %get-tuple-element.6.grad) | copy-start | bytes 98308

commit v4 on v3

--- a/solution.py
+++ b/solution.py
@@ -41,8 +41,6 @@
     residual_out,
     outgoing,
     incoming,
-    observed_halo,
-    background_halo,
     basis_here,
     observed_here,
     background_here,
@@ -54,8 +52,10 @@
     row_one,
     moved,
     edges,
-    middle,
+    core,
     light_halo,
+    edge_out,
+    edge_in,
     reach,
     windows,
     slot_grad,
@@ -156,30 +156,24 @@
             device_id_type=MESH,
         )
 
-    def halo_copies(upward):
+    def halo_copy(upward):
         other = me_s - 1 if upward else me_s + 1
-        start = 0 if upward else tile_rows - margin
         slot = 1 if upward else 0
-        return [
-            pltpu.make_async_remote_copy(
-                src_ref=array.at[0, pl.ds(start, margin)],
-                dst_ref=landing.at[slot],
-                send_sem=halo_send.at[which, slot],
-                recv_sem=halo_recv.at[which, slot],
-                device_id=(other, me_e),
-                device_id_type=MESH,
-            )
-            for which, (array, landing) in enumerate(
-                ((observed, observed_halo), (background, background_halo))
-            )
-        ]
+        return pltpu.make_async_remote_copy(
+            src_ref=edge_out.at[1 - slot],
+            dst_ref=edge_in.at[slot],
+            send_sem=halo_send.at[slot],
+            recv_sem=halo_recv.at[slot],
+            device_id=(other, me_e),
+            device_id_type=MESH,
+        )
 
     def light_copy(upward):
         other = me_s - 1 if upward else me_s + 1
-        start = 0 if upward else 2 * margin
+        start = 0 if upward else margin
         slot = 1 if upward else 0
         return pltpu.make_async_remote_copy(
-            src_ref=edges.at[pl.ds(start, 2 * margin)],
+            src_ref=edges.at[pl.ds(start, margin)],
             dst_ref=light_halo.at[slot],
             send_sem=light_send.at[slot],
             recv_sem=light_recv.at[slot],
@@ -190,14 +184,12 @@
     @pl.when(jnp.logical_not(has_above))
     def _():
         light_halo[0] = jnp.zeros(light_halo.shape[1:], jnp.float32)
-        observed_halo[0] = jnp.zeros(observed_halo.shape[1:], jnp.float32)
-        background_halo[0] = jnp.ones(background_halo.shape[1:], jnp.float32)
+        edge_in[0] = jnp.zeros(edge_in.shape[1:], jnp.bfloat16)
 
     @pl.when(jnp.logical_not(has_below))
     def _():
         light_halo[1] = jnp.zeros(light_halo.shape[1:], jnp.float32)
-        observed_halo[1] = jnp.zeros(observed_halo.shape[1:], jnp.float32)
-        background_halo[1] = jnp.ones(background_halo.shape[1:], jnp.float32)
+        edge_in[1] = jnp.zeros(edge_in.shape[1:], jnp.bfloat16)
 
     def natural(value):
         return 2 * (value & (half - 1)) + (value >> 5)
@@ -247,16 +239,6 @@
 
     for step in range(1, n_sky):
         param_copy(step).start()
-
-    @pl.when(has_above)
-    def _():
-        for copy in halo_copies(True):
-            copy.start()
-
-    @pl.when(has_below)
-    def _():
-        for copy in halo_copies(False):
-            copy.start()
 
     for load in loads[:4]:
         load.wait()
@@ -329,9 +311,9 @@
     lane_row = lax.broadcasted_iota(jnp.int32, (1, LANES), 1)
     level = lax.broadcasted_iota(jnp.int32, (canvas_rows, LANES), 0)
     level = jnp.where(
-        level < 2 * margin,
+        level < margin,
         level,
-        jnp.where(level < 4 * margin, level + (canvas_rows - 4 * margin), level - 2 * margin),
+        jnp.where(level < 2 * margin, level + tile_rows, level - margin),
     )
     offset = level - natural(lane_row & (size - 1))
     span = capacity * size
@@ -372,7 +354,7 @@
         first = wide_dot(row_one[rows, :run], moved[:run, :])
         return lax.fori_loop(1, n_sky * span // run, add, first)
 
-    edges[...] = gathered(slice(0, 4 * margin))
+    edges[...] = gathered(slice(0, 2 * margin))
 
     @pl.when(has_above)
     def _():
@@ -388,70 +370,70 @@
         numerator = jnp.where(image >= 0, 1.0, decay)
         return (seen - model) * numerator / (model * (1.0 + decay))
 
-    def keep(value, start):
-        rounded = value.astype(jnp.bfloat16).astype(jnp.float32)
+    def keep(rounded, start):
+        wide = rounded.astype(jnp.float32)
         for plane in range(planes):
-            reach[pl.ds(plane * canvas_rows + start, margin), :] = rounded[
+            reach[pl.ds(plane * canvas_rows + start, margin), :] = wide[
                 :, plane * LANES : (plane + 1) * LANES
             ]
 
-    middle[...] = gathered(slice(4 * margin, canvas_rows))
+    core[...] = gathered(slice(2 * margin, canvas_rows))
     for load in loads[4:]:
         load.wait()
 
+    def chunk_residual(start, light):
+        rows = pl.ds(start, margin)
+        image = core[rows, :] if light is None else core[rows, :] + light
+        value = residual_of(image, observed_here[rows, :], background_here[rows, :])
+        residual_out[0, rows, :] = value
+        rounded = value.astype(jnp.bfloat16)
+        keep(rounded, pl.multiple_of(start + margin, margin))
+        return rounded
+
     def core_chunk(index, carry):
-        start = pl.multiple_of(index * margin, margin)
-        inner = pl.multiple_of(start + margin, margin)
-        value = residual_of(
-            middle[pl.ds(start, margin), :],
-            observed_here[pl.ds(inner, margin), :],
-            background_here[pl.ds(inner, margin), :],
-        )
-        residual_out[0, pl.ds(inner, margin), :] = value
-        keep(value, pl.multiple_of(start + 2 * margin, margin))
+        chunk_residual(pl.multiple_of(index * margin, margin), None)
         return carry
 
-    lax.fori_loop(0, canvas_rows // margin - 4, core_chunk, 0, unroll=3)
+    chunks = tile_rows // margin
+    lax.fori_loop(1, chunks // 2, core_chunk, 0, unroll=3)
     reach[planes * canvas_rows :, :] = jnp.zeros((canvas_rows, LANES), jnp.float32)
 
     @pl.when(has_above)
     def _():
+        light_copy(False).wait_recv()
+
+    edge_out[0] = chunk_residual(0, light_halo[0])
+
+    @pl.when(has_above)
+    def _():
+        halo_copy(True).start()
+
+    @pl.when(has_below)
+    def _():
+        light_copy(True).wait_recv()
+
+    edge_out[1] = chunk_residual(tile_rows - margin, light_halo[1])
+
+    @pl.when(has_below)
+    def _():
+        halo_copy(False).start()
+
+    lax.fori_loop(chunks // 2, chunks - 1, core_chunk, 0, unroll=3)
+
+    @pl.when(has_above)
+    def _():
         light_copy(True).wait_send()
-        light_copy(False).wait_recv()
-        for copy in halo_copies(True):
-            copy.wait_send()
-        for copy in halo_copies(False):
-            copy.wait_recv()
+        halo_copy(True).wait_send()
+        halo_copy(False).wait_recv()
 
     @pl.when(has_below)
     def _():
         light_copy(False).wait_send()
-        light_copy(True).wait_recv()
-        for copy in halo_copies(False):
-            copy.wait_send()
-        for copy in halo_copies(True):
-            copy.wait_recv()
-
-    for slot, exists in ((0, has_above), (1, has_below)):
-        outer = 0 if slot == 0 else canvas_rows - margin
-        inner = margin if slot == 0 else canvas_rows - 2 * margin
-        outer_light = 0 if slot == 0 else margin
-        inner_light = margin - outer_light
-        value = residual_of(
-            edges[pl.ds(2 * slot * margin + outer_light, margin), :]
-            + light_halo[slot, pl.ds(outer_light, margin), :],
-            observed_halo[slot],
-            background_halo[slot],
-        )
-        keep(jnp.where(exists, value, 0.0), outer)
-        value = residual_of(
-            edges[pl.ds(2 * slot * margin + inner_light, margin), :]
-            + light_halo[slot, pl.ds(inner_light, margin), :],
-            observed_here[pl.ds(inner - margin, margin), :],
-            background_here[pl.ds(inner - margin, margin), :],
-        )
-        residual_out[0, pl.ds(inner - margin, margin), :] = value
-        keep(value, inner)
+        halo_copy(False).wait_send()
+        halo_copy(True).wait_recv()
+
+    keep(edge_in[0], 0)
+    keep(edge_in[1], canvas_rows - margin)
 
     def pick_owner(owner, carry):
         def pick(k, inner_carry):
@@ -623,8 +605,6 @@
         scratch_shapes=[
             pltpu.VMEM((n_sky, capacity, n_par), bf16),
             pltpu.VMEM((n_sky, capacity, n_par), bf16),
-            pltpu.VMEM((2, margin, width), f32),
-            pltpu.VMEM((2, margin, width), f32),
             pltpu.VMEM((n_par, pixels), bf16),
             pltpu.VMEM((tile_rows, width), f32),
             pltpu.VMEM((tile_rows, width), f32),
@@ -635,9 +615,11 @@
             pltpu.VMEM((pairs * (slots + 8), LANES), f32),
             pltpu.VMEM((canvas_rows, slots * size), bf16),
             pltpu.VMEM((slots * size, width), bf16),
-            pltpu.VMEM((4 * margin, width), f32),
-            pltpu.VMEM((tile_rows - 2 * margin, width), f32),
-            pltpu.VMEM((2, 2 * margin, width), f32),
+            pltpu.VMEM((2 * margin, width), f32),
+            pltpu.VMEM((tile_rows, width), f32),
+            pltpu.VMEM((2, margin, width), f32),
+            pltpu.VMEM((2, margin, width), bf16),
+            pltpu.VMEM((2, margin, width), bf16),
             pltpu.VMEM(((planes + 1) * canvas_rows, LANES), f32),
             pltpu.VMEM((slots, pixels), bf16),
             pltpu.VMEM((slots, n_par), f32),
@@ -647,8 +629,8 @@
             dma((6,)),
             dma((n_sky,)),
             dma((n_sky,)),
-            dma((2, 2)),
-            dma((2, 2)),
+            dma((2,)),
+            dma((2,)),
             dma((2,)),
             dma((2,)),
             dma((n_epoch,)),
@@ -680,6 +662,7 @@
         in_specs=[vmem, vmem],
         out_specs=(hbm, hbm),
         scratch_shapes=[dma((5,))],
+        compiler_params=pltpu.CompilerParams(vmem_limit_bytes=2 * 1024 * 1024),
     )(param_grad, residual)
     return param_grad.T, residual
 

time: 34.8 us -> 33.2 us (0.954)
  local copies, waits for them, and re-layouts: 1.38 us -> 0 us
    unnamed x4 -> x0, local copies, waits for them, and re-layouts: 1.38 us -> none
    pallas_call x1, Pallas kernels: 1.89 us -> 0.83 us  [on_device(): pl.pallas_call(finish, out_shape=(jax.ShapeDtypeStruct(param_grad.shape,...]
    pallas_call x1, Pallas kernels: 30.7 us -> 31.5 us  [on_device(): pl.pallas_call(functools.partial(kernel, n_sky, n_epoch), out_shape=(jax....]
where the time goes in v4:
time: 33.2 us; the launch traced here: 33 us
  Pallas kernels  32.4 us (98%)
  between operations  0.64 us (2%)
    pallas_call x1, Pallas kernels, on_device(): pl.pallas_call(functools.partial(kernel, n_sky, n_epoch), out_shape=(jax....  31.5 us
    pallas_call x1, Pallas kernels, on_device(): pl.pallas_call(finish, out_shape=(jax.ShapeDtypeStruct(param_grad.shape,...  0.83 us

profile of v4, /device:TPU:0, one launch (start us, length us, event | category | flops | bytes accessed | tf_op | source)
XLA Modules:
  0.0 33.0 jit_solution(14439559769739283221)
XLA Ops:
  0.6 31.5 %shard_map.104 = (f32[64,128]{1,0:T(8,128)S(1)}, f32[1,256,512]{2,1,0:T(8,128)S(1)}) custom-call(bf16[64,128]{1,0:T(8,128)(2,1)} %bitcast.2, bf16[64,4096]{1,0:T(8,128)(2,1)} %basis.1, f32[1,2,51]{2,1,0:T(2,128)} %taps_vector.1, f32[1,2,51]{2,1,0:T(2,128)} %taps_vector.1, s32[1,4,16]{2,1,0:T(4,128)} %send_index.1, s32[1,4]{1,0:T(1,128)} %tile_count.1, ...), custom_call_target="tpu_custom_call" | custom-call | tf_op jit(solution)/shard_map/pallas_call | solution.py:597
  32.2 0.8 %shard_map.105 = (f32[64,128]{1,0:T(8,128)}, f32[1,256,512]{2,1,0:T(8,128)}) custom-call(f32[64,128]{1,0:T(8,128)S(1)} %get-tuple-element.6.grad, f32[1,256,512]{2,1,0:T(8,128)S(1)} %get-tuple-element.7.residual), custom_call_target="tpu_custom_call" | custom-call | tf_op jit(solution)/shard_map/pallas_call | solution.py:656

commit v5 on v3

--- a/solution.py
+++ b/solution.py
@@ -59,7 +59,7 @@
     reach,
     windows,
     slot_grad,
-    reduce_in,
+    part_in,
     piece,
     gather_in,
     load_sem,
@@ -69,8 +69,8 @@
     halo_recv,
     light_send,
     light_recv,
-    reduce_send,
-    reduce_recv,
+    part_send,
+    part_recv,
     gather_send,
     gather_recv,
 ):
@@ -87,11 +87,11 @@
     canvas_rows = tile_rows + 2 * margin
     planes = width // LANES
     pairs = size * size // LANES
-    per = slots // n_epoch
-    ratio = capacity // per
+    per = capacity // 2
     n_taps = taps_vector.shape[2]
     reach_taps = (n_taps - 1) // 2
-    my_owner = me_e // ratio
+    me_core = lax.rem(me_e, 2)
+    sibling = me_e + 1 - 2 * me_core
     slot_pitch = slots + 8
     par_pitch = n_par + 8
     has_above = me_s > 0
@@ -112,21 +112,18 @@
         load.start()
 
     barrier = pltpu.get_barrier_semaphore()
-    for step in range(1, n_sky):
+    for step in range(n_sky):
+        for other in (me_e, sibling)[int(step == 0) :]:
+            pl.semaphore_signal(
+                barrier, 1, device_id=(wrapped(me_s + step, n_sky), other), device_id_type=MESH
+            )
+    for step in range(2, n_epoch):
         pl.semaphore_signal(
-            barrier, 1, device_id=(wrapped(me_s + step, n_sky), me_e), device_id_type=MESH
-        )
-    for step in range(1, n_epoch):
-        pl.semaphore_signal(
-            barrier, 1, device_id=(me_s, wrapped(me_e + step, n_epoch)), device_id_type=MESH
-        )
-    for tile in range(n_sky):
-        for part in range(ratio):
-            sender = me_s * ratio + part
-
-            @pl.when(jnp.logical_not((me_s == tile) & (sender == me_e)))
-            def _():
-                pl.semaphore_signal(barrier, 1, device_id=(tile, sender), device_id_type=MESH)
+            barrier,
+            1,
+            device_id=(me_s, wrapped(me_e - me_core + step, n_epoch)),
+            device_id_type=MESH,
+        )
 
     slot_at = lax.broadcasted_iota(jnp.int32, (8, n_source), 0)
     source_at = lax.broadcasted_iota(jnp.int32, (8, n_source), 1)
@@ -240,11 +237,7 @@
         axis=0,
     )
 
-    pl.semaphore_wait(
-        barrier,
-        (n_sky - 1) + (n_epoch - 1) + n_epoch - jnp.where(my_owner == me_s, 1, 0),
-    )
-
+    pl.semaphore_wait(barrier, (2 * n_sky - 1) + (n_epoch - 2))
     for step in range(1, n_sky):
         param_copy(step).start()
 
@@ -334,6 +327,8 @@
         jnp.where(level < 4 * margin, level + (canvas_rows - 4 * margin), level - 2 * margin),
     )
     offset = level - natural(lane_row & (size - 1))
+    offset = jnp.where(offset < 0, -1, jnp.where(offset > tile_rows, 2 * tile_rows, offset))
+    offset = offset.astype(jnp.float32).astype(jnp.bfloat16)
     span = capacity * size
 
     def place_owner(owner, carry):
@@ -346,19 +341,21 @@
                 rows.append(stamp_row[0, owner, k])
                 stamp = stamps[pl.ds(owner * capacity + k, half, stride=slot_pitch), :]
                 even = pltpu.roll(stamp, col & (LANES - 1), 1)
-                odd = pltpu.roll(even, size, 1)
+                odd = pltpu.roll(even, size, 1).astype(jnp.bfloat16)
+                even = even.astype(jnp.bfloat16)
                 for plane in range(planes):
                     at = lane_row + (plane * LANES) - col
-                    inside = (at >= 0) & (at < size)
+                    inside = jnp.where((at >= 0) & (at < size), 1.0, 0.0).astype(jnp.bfloat16)
                     for parity, data in enumerate((even, odd)):
                         moved[
                             pl.ds(base + k * size + parity * half, half),
                             plane * LANES : (plane + 1) * LANES,
-                        ] = jnp.where(inside, data, 0.0).astype(jnp.bfloat16)
+                        ] = data * inside
             target = jnp.where(lane_row < size, rows[0], rows[1])
+            target = target.astype(jnp.float32).astype(jnp.bfloat16)
             row_one[:, pl.ds(base + pair * LANES, LANES)] = jnp.where(
-                offset == target, 1.0, 0.0
-            ).astype(jnp.bfloat16)
+                offset == target, jnp.ones_like(offset), jnp.zeros_like(offset)
+            )
         return carry
 
     lax.fori_loop(0, n_sky, place_owner, 0)
@@ -466,7 +463,7 @@
                 far = reach[pl.ds(first + canvas_rows + parity, half, stride=2), :]
                 halves.append(jnp.where(lane_row >= shift, near, far))
             even = pltpu.roll(halves[0], back, 1)
-            odd = pltpu.roll(pltpu.roll(halves[1], back, 1), size, 1)
+            odd = pltpu.roll(halves[1], (LANES + size - shift) & (LANES - 1), 1)
             stamps[pl.ds(owner * capacity + k, half, stride=slot_pitch), :] = jnp.where(
                 lane_half, even, odd
             )
@@ -482,71 +479,63 @@
     both = wide_dot(windows[...], rendered[...], (((1,), (1,)), ((), ())))
     slot_grad[...] = jnp.where(live > 0, both[:, :n_par] + both[:, n_par:], 0.0)
 
-    def reduce_copy(step):
-        other = wrapped(me_e + step, n_epoch)
+    def part_copy(step, cross):
+        owner = wrapped(me_s + step, n_sky)
+        core = 1 - me_core if cross else me_core
+        start = pl.multiple_of(owner * capacity + core * per, per)
         return pltpu.make_async_remote_copy(
-            src_ref=slot_grad.at[pl.ds(pl.multiple_of(other * per, per), per)],
-            dst_ref=reduce_in.at[step],
-            send_sem=reduce_send.at[step],
-            recv_sem=reduce_recv.at[step],
-            device_id=(me_s, other),
+            src_ref=slot_grad.at[pl.ds(start, per)],
+            dst_ref=part_in.at[me_s, me_core],
+            send_sem=part_send.at[step, cross],
+            recv_sem=part_recv.at[step, cross],
+            device_id=(owner, sibling if cross else me_e),
             device_id_type=MESH,
         )
 
-    for step in range(1, n_epoch):
-        reduce_copy(step).start()
-    summed = slot_grad[pl.ds(pl.multiple_of(me_e * per, per), per), :]
-    for step in range(1, n_epoch):
-        reduce_copy(step).wait_recv()
-        summed = summed + reduce_in[step]
-    piece[...] = summed
-    my_place = me_s * ratio + lax.rem(me_e, ratio)
+    parts = [(step, cross) for step in range(n_sky) for cross in range(2)][1:]
+    for part in parts:
+        part_copy(*part).start()
+    start = pl.multiple_of(me_s * capacity + me_core * per, per)
+    part_in[me_s, me_core] = slot_grad[pl.ds(start, per), :]
+    for part in parts:
+        part_copy(*part).wait_recv()
+    both_cores = (part_in[:, 0] + part_in[:, 1]).reshape(n_sky * per, n_par)
+    fold = n_sky * per // 2
+    piece[...] = jnp.concatenate([both_cores[:fold], both_cores[fold:]], axis=1)
 
     def gather_copy(step):
         return pltpu.make_async_remote_copy(
             src_ref=piece,
-            dst_ref=gather_in.at[my_place],
+            dst_ref=gather_in.at[me_e],
             send_sem=gather_send.at[step],
-            recv_sem=gather_recv.at[my_place],
-            device_id=(my_owner, wrapped(me_e + step, n_epoch)),
+            recv_sem=gather_recv.at[step],
+            device_id=(me_s, wrapped(me_e + step, n_epoch)),
             device_id_type=MESH,
         )
 
     for step in range(1, n_epoch):
         gather_copy(step).start()
-
-    @pl.when(my_owner == me_s)
-    def _():
-        gather_in[my_place] = piece[...]
-
-    @pl.when(my_owner != me_s)
-    def _():
-        gather_copy(0).start()
-
+    gather_in[me_e] = piece[...]
+    for part in parts:
+        part_copy(*part).wait_send()
     for step in range(1, n_epoch):
-        reduce_copy(step).wait_send()
-        gather_copy(step).wait_send()
-
-    @pl.when(my_owner != me_s)
-    def _():
-        gather_copy(0).wait_send()
-
-    for tile in range(n_sky):
-        for part in range(ratio):
-
-            @pl.when(jnp.logical_not((me_s == tile) & (me_s * ratio + part == me_e)))
-            def _():
-                place = tile * ratio + part
-                pltpu.make_async_remote_copy(
-                    src_ref=piece,
-                    dst_ref=gather_in.at[place],
-                    send_sem=gather_send.at[0],
-                    recv_sem=gather_recv.at[place],
-                    device_id=(tile, me_s * ratio + part),
-                    device_id_type=MESH,
-                ).wait_recv()
-
-    back = gather_in[...].reshape(slots, n_par)
+        gather_copy(step).wait()
+    summed = []
+    for core in range(2):
+        total = gather_in[core]
+        for chip in range(1, n_epoch // 2):
+            total = total + gather_in[2 * chip + core]
+        summed.extend([total[:, :n_par], total[:, n_par:]])
+    back = jnp.concatenate(summed, axis=0)
+    table = jnp.concatenate(
+        [
+            rows_of[(tile * capacity + core * per + base) // 8]
+            for core in range(2)
+            for tile in range(n_sky)
+            for base in range(0, per, 8)
+        ],
+        axis=0,
+    )
     high = back.astype(jnp.bfloat16)
     rest = back - high.astype(jnp.float32)
     middle_part, low = split_two(rest)
@@ -597,8 +586,7 @@
     canvas_rows = tile_rows + 2 * margin
     planes = width // LANES
     pairs = pixels // LANES
-    per = slots // n_epoch
-    ratio = capacity // per
+    per = capacity // 2
     f32, bf16 = jnp.float32, jnp.bfloat16
     vmem = pl.BlockSpec(memory_space=pltpu.VMEM)
     smem = pl.BlockSpec(memory_space=pltpu.SMEM)
@@ -641,9 +629,9 @@
             pltpu.VMEM(((planes + 1) * canvas_rows, LANES), f32),
             pltpu.VMEM((slots, pixels), bf16),
             pltpu.VMEM((slots, n_par), f32),
-            pltpu.VMEM((n_epoch, per, n_par), f32),
-            pltpu.VMEM((per, n_par), f32),
-            pltpu.VMEM((n_sky * ratio, per, n_par), f32),
+            pltpu.VMEM((n_sky, 2, per, n_par), f32),
+            pltpu.VMEM((n_sky * per // 2, 2 * n_par), f32),
+            pltpu.VMEM((n_epoch, n_sky * per // 2, 2 * n_par), f32),
             dma((6,)),
             dma((n_sky,)),
             dma((n_sky,)),
@@ -651,10 +639,10 @@
             dma((2, 2)),
             dma((2,)),
             dma((2,)),
+            dma((n_sky, 2)),
+            dma((n_sky, 2)),
             dma((n_epoch,)),
             dma((n_epoch,)),
-            dma((n_epoch,)),
-            dma((n_sky * ratio,)),
         ],
         compiler_params=pltpu.CompilerParams(
             collective_id=0, has_side_effects=True, vmem_limit_bytes=(14 * 1024 + slots * 160) * 1024
@@ -680,6 +668,7 @@
         in_specs=[vmem, vmem],
         out_specs=(hbm, hbm),
         scratch_shapes=[dma((5,))],
+        compiler_params=pltpu.CompilerParams(vmem_limit_bytes=2 * 1024 * 1024),
     )(param_grad, residual)
     return param_grad.T, residual
 

time: 34.8 us -> 30.7 us (0.88)
  Pallas kernels: 32.5 us -> 29.9 us
  local copies, waits for them, and re-layouts: 1.38 us -> 0 us
    pallas_call x1, Pallas kernels: 30.7 us -> 29 us  [on_device(): pl.pallas_call(functools.partial(kernel, n_sky, n_epoch), out_shape=(jax....]
    unnamed x4 -> x0, local copies, waits for them, and re-layouts: 1.38 us -> none
    pallas_call x1, Pallas kernels: 1.89 us -> 0.83 us  [on_device(): pl.pallas_call(finish, out_shape=(jax.ShapeDtypeStruct(param_grad.shape,...]
where the time goes in v5:
time: 30.7 us; the launch traced here: 30.5 us
  Pallas kernels  29.9 us (97%)
  between operations  0.64 us (2%)
    pallas_call x1, Pallas kernels, on_device(): pl.pallas_call(functools.partial(kernel, n_sky, n_epoch), out_shape=(jax....  29 us
    pallas_call x1, Pallas kernels, on_device(): pl.pallas_call(finish, out_shape=(jax.ShapeDtypeStruct(param_grad.shape,...  0.83 us

profile of v5, /device:TPU:0, one launch (start us, length us, event | category | flops | bytes accessed | tf_op | source)
XLA Modules:
  0.0 30.5 jit_solution(17337752392010034492)
XLA Ops:
  0.6 29.0 %shard_map.104 = (f32[64,128]{1,0:T(8,128)S(1)}, f32[1,256,512]{2,1,0:T(8,128)S(1)}) custom-call(bf16[64,128]{1,0:T(8,128)(2,1)} %bitcast.2, bf16[64,4096]{1,0:T(8,128)(2,1)} %basis.1, f32[1,2,51]{2,1,0:T(2,128)} %taps_vector.1, f32[1,2,51]{2,1,0:T(2,128)} %taps_vector.1, s32[1,4,16]{2,1,0:T(4,128)} %send_index.1, s32[1,4]{1,0:T(1,128)} %tile_count.1, ...), custom_call_target="tpu_custom_call" | custom-call | tf_op jit(solution)/shard_map/pallas_call | solution.py:603
  29.7 0.8 %shard_map.105 = (f32[64,128]{1,0:T(8,128)}, f32[1,256,512]{2,1,0:T(8,128)}) custom-call(f32[64,128]{1,0:T(8,128)S(1)} %get-tuple-element.6.grad, f32[1,256,512]{2,1,0:T(8,128)S(1)} %get-tuple-element.7.residual), custom_call_target="tpu_custom_call" | custom-call | tf_op jit(solution)/shard_map/pallas_call | solution.py:662

commit v6 on v5

--- a/solution.py
+++ b/solution.py
@@ -50,6 +50,7 @@
     basis_mixed,
     rendered_rows,
     rendered,
+    rendered_turned,
     stamps,
     row_one,
     moved,
@@ -171,18 +172,21 @@
             )
         ]
 
-    def light_copy(upward):
+    def light_copies(upward):
         other = me_s - 1 if upward else me_s + 1
         start = 0 if upward else 2 * margin
         slot = 1 if upward else 0
-        return pltpu.make_async_remote_copy(
-            src_ref=edges.at[pl.ds(start, 2 * margin)],
-            dst_ref=light_halo.at[slot],
-            send_sem=light_send.at[slot],
-            recv_sem=light_recv.at[slot],
-            device_id=(other, me_e),
-            device_id_type=MESH,
-        )
+        return [
+            pltpu.make_async_remote_copy(
+                src_ref=edges.at[pl.ds(start + part * margin, margin)],
+                dst_ref=light_halo.at[slot, pl.ds(part * margin, margin)],
+                send_sem=light_send.at[slot, part],
+                recv_sem=light_recv.at[slot, part],
+                device_id=(other, me_e),
+                device_id_type=MESH,
+            )
+            for part in range(2)
+        ]
 
     @pl.when(jnp.logical_not(has_above))
     def _():
@@ -329,7 +333,13 @@
     offset = level - natural(lane_row & (size - 1))
     offset = jnp.where(offset < 0, -1, jnp.where(offset > tile_rows, 2 * tile_rows, offset))
     offset = offset.astype(jnp.float32).astype(jnp.bfloat16)
+    edge_offset = offset[: 4 * margin]
+    core_offset = offset[4 * margin :]
     span = capacity * size
+
+    def target_rows(rows):
+        target = jnp.where(lane_row < size, rows[0], rows[1])
+        return target.astype(jnp.float32).astype(jnp.bfloat16)
 
     def place_owner(owner, carry):
         base = pl.multiple_of(owner * span, span)
@@ -351,10 +361,9 @@
                             pl.ds(base + k * size + parity * half, half),
                             plane * LANES : (plane + 1) * LANES,
                         ] = data * inside
-            target = jnp.where(lane_row < size, rows[0], rows[1])
-            target = target.astype(jnp.float32).astype(jnp.bfloat16)
-            row_one[:, pl.ds(base + pair * LANES, LANES)] = jnp.where(
-                offset == target, jnp.ones_like(offset), jnp.zeros_like(offset)
+            target = target_rows(rows)
+            row_one[: 4 * margin, pl.ds(base + pair * LANES, LANES)] = jnp.where(
+                edge_offset == target, jnp.ones_like(edge_offset), jnp.zeros_like(edge_offset)
             )
         return carry
 
@@ -373,11 +382,13 @@
 
     @pl.when(has_above)
     def _():
-        light_copy(True).start()
+        for copy in light_copies(True):
+            copy.start()
 
     @pl.when(has_below)
     def _():
-        light_copy(False).start()
+        for copy in light_copies(False):
+            copy.start()
 
     def residual_of(image, seen, sky):
         decay = jnp.exp(-jnp.abs(image))
@@ -392,6 +403,16 @@
                 :, plane * LANES : (plane + 1) * LANES
             ]
 
+    def middle_owner(owner, carry):
+        base = pl.multiple_of(owner * span, span)
+        for pair in range(capacity // 2):
+            target = target_rows([stamp_row[0, owner, 2 * pair + which] for which in range(2)])
+            row_one[4 * margin :, pl.ds(base + pair * LANES, LANES)] = jnp.where(
+                core_offset == target, jnp.ones_like(core_offset), jnp.zeros_like(core_offset)
+            )
+        return carry
+
+    lax.fori_loop(0, n_sky, middle_owner, 0)
     middle[...] = gathered(slice(4 * margin, canvas_rows))
     for load in loads[4:]:
         load.wait()
@@ -411,10 +432,17 @@
     lax.fori_loop(0, canvas_rows // margin - 4, core_chunk, 0, unroll=3)
     reach[planes * canvas_rows :, :] = jnp.zeros((canvas_rows, LANES), jnp.float32)
 
+    for pair in range(pairs):
+        rendered_turned[pair * LANES : (pair + 1) * LANES, :] = rendered[
+            :, pair * LANES : (pair + 1) * LANES
+        ].T
+
     @pl.when(has_above)
     def _():
-        light_copy(True).wait_send()
-        light_copy(False).wait_recv()
+        for copy in light_copies(True):
+            copy.wait_send()
+        for copy in light_copies(False):
+            copy.wait_recv()
         for copy in halo_copies(True):
             copy.wait_send()
         for copy in halo_copies(False):
@@ -422,8 +450,10 @@
 
     @pl.when(has_below)
     def _():
-        light_copy(False).wait_send()
-        light_copy(True).wait_recv()
+        for copy in light_copies(False):
+            copy.wait_send()
+        for copy in light_copies(True):
+            copy.wait_recv()
         for copy in halo_copies(False):
             copy.wait_send()
         for copy in halo_copies(True):
@@ -476,7 +506,7 @@
         windows[:, pair * LANES : (pair + 1) * LANES] = stamps[
             pl.ds(pair * slot_pitch, slots), :
         ].astype(jnp.bfloat16)
-    both = wide_dot(windows[...], rendered[...], (((1,), (1,)), ((), ())))
+    both = wide_dot(windows[...], rendered_turned[...])
     slot_grad[...] = jnp.where(live > 0, both[:, :n_par] + both[:, n_par:], 0.0)
 
     def part_copy(step, cross):
@@ -620,6 +650,7 @@
             pltpu.VMEM((size, pixels), bf16),
             pltpu.VMEM((pairs * (n_par + 8), LANES), f32),
             pltpu.VMEM((2 * n_par, pixels), bf16),
+            pltpu.VMEM((pixels, 2 * n_par), bf16),
             pltpu.VMEM((pairs * (slots + 8), LANES), f32),
             pltpu.VMEM((canvas_rows, slots * size), bf16),
             pltpu.VMEM((slots * size, width), bf16),
@@ -637,8 +668,8 @@
             dma((n_sky,)),
             dma((2, 2)),
             dma((2, 2)),
-            dma((2,)),
-            dma((2,)),
+            dma((2, 2)),
+            dma((2, 2)),
             dma((n_sky, 2)),
             dma((n_sky, 2)),
             dma((n_epoch,)),

time: 30.7 us -> 30.3 us (0.987)
  Pallas kernels: 29.9 us -> 29.5 us
    pallas_call x1, Pallas kernels: 29 us -> 28.7 us  [on_device(): pl.pallas_call(functools.partial(kernel, n_sky, n_epoch), out_shape=(jax....]
where the time goes in v6:
time: 30.3 us; the launch traced here: 30.2 us
  Pallas kernels  29.5 us (97%)
  between operations  0.64 us (2%)
    pallas_call x1, Pallas kernels, on_device(): pl.pallas_call(functools.partial(kernel, n_sky, n_epoch), out_shape=(jax....  28.7 us
    pallas_call x1, Pallas kernels, on_device(): pl.pallas_call(finish, out_shape=(jax.ShapeDtypeStruct(param_grad.shape,...  0.83 us

profile of v6, /device:TPU:0, one launch (start us, length us, event | category | flops | bytes accessed | tf_op | source)
XLA Modules:
  0.0 30.2 jit_solution(12623750593676053532)
XLA Ops:
  0.6 28.7 %shard_map.104 = (f32[64,128]{1,0:T(8,128)S(1)}, f32[1,256,512]{2,1,0:T(8,128)S(1)}) custom-call(bf16[64,128]{1,0:T(8,128)(2,1)} %bitcast.2, bf16[64,4096]{1,0:T(8,128)(2,1)} %basis.1, f32[1,2,51]{2,1,0:T(2,128)} %taps_vector.1, f32[1,2,51]{2,1,0:T(2,128)} %taps_vector.1, s32[1,4,16]{2,1,0:T(4,128)} %send_index.1, s32[1,4]{1,0:T(1,128)} %tile_count.1, ...), custom_call_target="tpu_custom_call" | custom-call | tf_op jit(solution)/shard_map/pallas_call | solution.py:633
  29.3 0.8 %shard_map.105 = (f32[64,128]{1,0:T(8,128)}, f32[1,256,512]{2,1,0:T(8,128)}) custom-call(f32[64,128]{1,0:T(8,128)S(1)} %get-tuple-element.6.grad, f32[1,256,512]{2,1,0:T(8,128)S(1)} %get-tuple-element.7.residual), custom_call_target="tpu_custom_call" | custom-call | tf_op jit(solution)/shard_map/pallas_call | solution.py:693
